TPU v7x, 32 devices: a whole 2x2x4 slice. The times are simulated.
32 devices in a mesh: ctx: 16 (over z, x, core), tp: 2 (over y).
Axes of the slice: x: 2, y: 2, z: 4, core: 2. Of those that a mesh axis runs over, the one named last changes fastest.
Arguments:
- record_lengths: int32 [16], replicated, may hold values from 1 to 1728, 3072 in all
- query_heads: bfloat16 [3072, 8192], P(('ctx', 'tp')), may hold values from -36 to 36
- key_heads: bfloat16 [3072, 1024], P(('ctx', 'tp')), may hold values from -36 to 36
- value_heads: bfloat16 [3072, 1024], P(('ctx', 'tp')), may hold values from -5 to 5
- out_grad: bfloat16 [3072, 8192], P(('ctx', 'tp')), may hold values from -5 to 5
- gate_input: bfloat16 [3072, 8192], P('ctx', 'tp'), may hold values from -5 to 5
- key_input: bfloat16 [3072, 8192], P('ctx', 'tp'), may hold values from -5 to 5
- value_input: bfloat16 [3072, 8192], P('ctx', 'tp'), may hold values from -5 to 5
- hyena_grad: bfloat16 [3072, 8192], P('ctx', 'tp'), may hold values from -5 to 5
- short_filter: float32 [3, 3, 8192], P(None, None, 'tp'), may hold values from -3 to 3
- long_filter: float32 [7, 512], P(None, 'tp'), may hold values from -3 to 3
Outputs:
- attn_out: bfloat16 [3072, 8192], P('ctx', 'tp')
- grad_query: bfloat16 [3072, 8192], P('ctx', 'tp')
- grad_key: bfloat16 [3072, 1024], P('ctx', 'tp')
- grad_value: bfloat16 [3072, 1024], P('ctx', 'tp')
- hyena_out: bfloat16 [3072, 8192], P('ctx', 'tp')
- grad_gate_in: bfloat16 [3072, 8192], P('ctx', 'tp')
- grad_key_in: bfloat16 [3072, 8192], P('ctx', 'tp')
- grad_value_in: bfloat16 [3072, 8192], P('ctx', 'tp')
Inputs may be any that keep to these rules, and one draw needn't show every extreme that they name: `record_lengths`: the 16 records lie end to end and fill the 3072 tokens; the longest has exactly 1728 tokens.
All inputs are finite; a program needn't handle non-finite values.
Results may differ from a plain program's by a relative error of at most 0.035.
Values may be sent and summed in bfloat16 or wider, within the bound.
No kernel may reach another device: no remote copies, remote signals or barrier semaphores. Data moves between devices by JAX's collectives and lax.ppermute only.
A program may use at most 128 MiB of HBM per device.

v0:
```python
import functools

import jax
import jax.numpy as jnp
import numpy as np
from jax import lax
from jax.experimental import pallas as pl
from jax.experimental.pallas import tpu as pltpu
from jax.sharding import PartitionSpec as P

HD = 128
QH = 64
KVH = 8
GROUP = 16
TAPS = 7
SHORT = 3
HALO = 8
PLANE = 4
KB = 256
NEG = -1e30
SCALE = HD ** (-0.5)
TO_EXP2 = SCALE * 1.4426950408889634
VMEM = 48 * 1024 * 1024
VMEM_PACK = 62 * 1024 * 1024


def hyena_kernel(
    first,
    gate_ref,
    key_ref,
    value_ref,
    grad_ref,
    inner_ref,
    outer_ref,
    short_ref,
    long_ref,
    *refs,
):
    out_ref, dgate_ref, dkey_ref, dvalue_ref, taps, shift = refs[-6:]
    tokens, width = gate_ref.shape
    own = pl.program_id(0)
    odd = lax.axis_index("ctx") % 2

    @pl.when(own == 0)
    def _():
        shape = (long_ref.shape[1], taps.shape[1])
        group = lax.broadcasted_iota(jnp.int32, shape, 0)
        channel = first + lax.broadcasted_iota(jnp.int32, shape, 1)
        taps[...] = jnp.dot(
            long_ref[...],
            (group == channel // GROUP).astype(jnp.float32),
            precision=lax.Precision.HIGHEST,
            preferred_element_type=jnp.float32,
        )

    rows = tokens + 2 * HALO

    def chunk(index, carry):
        lanes = pl.ds(pl.multiple_of(index * HD, HD), HD)
        inner = inner_ref[:, lanes].astype(jnp.float32)
        outer = outer_ref[:, lanes].astype(jnp.float32)
        before = jnp.where(odd == 1, inner, outer)
        after = jnp.where(odd == 1, outer, inner)

        long = taps[:, pl.ds(pl.multiple_of(own * width + index * HD, HD), HD)]

        def short(which, tap):
            return short_ref[which, tap : tap + 1, lanes]

        def hold(slot, values, first=0):
            shift[slot, first + HALO : first + HALO + values.shape[0]] = values

        def at(slot, first, count):
            return shift[slot, first + HALO : first + HALO + count]

        def padded(ref, which):
            part = slice(which * HALO, (which + 1) * HALO)
            return jnp.concatenate(
                [before[part], ref[:, lanes].astype(jnp.float32), after[part]], axis=0
            )

        def featurize(ref, which):
            values = padded(ref, which)
            hold(which, values)
            result = short(which, 0) * values
            for tap in range(1, SHORT):
                result = result + short(which, tap) * at(which, -tap, rows)
            return result

        def unfeaturize(grads, which):
            hold(which, grads, HALO)
            result = short(which, 0) * grads[:tokens]
            for tap in range(1, SHORT):
                result = result + short(which, tap) * at(which, HALO + tap, tokens)
            return result.astype(jnp.bfloat16)

        count = tokens + HALO
        key_f = featurize(key_ref, 1)
        value_f = featurize(value_ref, 2)
        mixed = key_f * value_f
        hold(3, mixed)
        conv = long[0:1] * mixed[HALO:]
        for tap in range(1, TAPS):
            conv = conv + long[tap : tap + 1] * at(3, HALO - tap, count)
        gate_f = featurize(gate_ref, 0)[HALO:]
        out_ref[:, lanes] = (gate_f * conv)[:tokens].astype(jnp.bfloat16)
        grad = padded(grad_ref, 3)[HALO:]
        dgate_ref[:, lanes] = unfeaturize(grad * conv, 0)
        dconv = grad * gate_f
        hold(4, dconv, HALO)
        dmixed = long[0:1] * dconv
        for tap in range(1, TAPS):
            dmixed = dmixed + long[tap : tap + 1] * at(4, HALO + tap, count)
        dkey_ref[:, lanes] = unfeaturize(dmixed * value_f[HALO:], 1)
        dvalue_ref[:, lanes] = unfeaturize(dmixed * key_f[HALO:], 2)
        return carry

    lax.fori_loop(0, width // HD, chunk, 0)


def hyena(streams, inner, outer, short_filter, long_filter, first, steps, filled=()):
    tokens, channels = streams[0].shape
    width = channels // 8
    own = steps * width
    block = pl.BlockSpec((tokens, width), lambda i: (0, first + i))
    edge = pl.BlockSpec((4 * HALO, width), lambda i: (0, first + i))
    return pl.pallas_call(
        functools.partial(hyena_kernel, first * width),
        grid=(steps,),
        in_specs=[block] * 4
        + [edge, edge]
        + [
            pl.BlockSpec((3, SHORT, width), lambda i: (0, 0, first + i)),
            pl.BlockSpec(long_filter.shape, lambda i: (0, 0)),
        ]
        + [pl.BlockSpec(memory_space=pl.ANY)] * len(filled),
        out_specs=[block] * 4,
        out_shape=[jax.ShapeDtypeStruct((tokens, channels), jnp.bfloat16)] * 4,
        scratch_shapes=[
            pltpu.VMEM((TAPS, own), jnp.float32),
            pltpu.VMEM((5, tokens + 4 * HALO, HD), jnp.float32),
        ],
        input_output_aliases={8 + i: i for i in range(len(filled))},
        compiler_params=pltpu.CompilerParams(vmem_limit_bytes=VMEM),
        cost_estimate=pl.CostEstimate(
            flops=14000 * tokens * own, bytes_accessed=16 * tokens * own, transcendentals=0
        ),
        name="hyena",
    )(*streams, inner, outer, short_filter, long_filter, *filled)


def own_slot(split):
    return lax.axis_index("tp") * split + lax.axis_index("ctx") % split


def pack_edges_kernel(k_ref, v_ref, *refs):
    streams = (len(refs) - 3) // 2
    first_refs, last_refs = refs[:streams], refs[streams : 2 * streams]
    kv_ref, inner_ref, outer_ref = refs[2 * streams :]
    width = kv_ref.shape[3]
    for slot in range(kv_ref.shape[0]):
        part = slice(slot * width, (slot + 1) * width)
        kv_ref[slot, 0] = k_ref[:, part]
        kv_ref[slot, 1] = v_ref[:, part]
    f32 = jnp.float32
    odd = lax.axis_index("ctx") % 2

    def edge(refs, start, at):
        pair = [ref[...].astype(f32)[start : start + HALO] for ref in refs[at : at + 2]]
        return jnp.concatenate(pair, axis=0)

    for at in range(0, streams, 2):
        rows = slice(at * HALO, (at + 2) * HALO)
        head, tail = edge(first_refs, 0, at), edge(last_refs, HALO, at)
        inner_ref[rows] = jnp.where(odd == 1, head, tail).astype(inner_ref.dtype)
        outer_ref[rows] = jnp.where(odd == 1, tail, head).astype(outer_ref.dtype)


def pack_edges(keys, values, streams, slots):
    rows, columns = keys.shape
    tokens, channels = streams[0].shape
    edge = 2 * HALO
    count = len(streams)
    whole = pl.BlockSpec((rows, columns), lambda i: (0, 0))
    first = pl.BlockSpec((edge, channels), lambda i: (0, 0))
    last = pl.BlockSpec((edge, channels), lambda i: (tokens // edge - 1, 0))
    halo = (count * HALO, channels)
    laid = (slots, 2, rows, columns // slots)
    return pl.pallas_call(
        pack_edges_kernel,
        grid=(1,),
        in_specs=[whole] * 2 + [first] * count + [last] * count,
        out_specs=[
            pl.BlockSpec(laid, lambda i: (0, 0, 0, 0)),
            pl.BlockSpec(halo, lambda i: (0, 0)),
            pl.BlockSpec(halo, lambda i: (0, 0)),
        ],
        out_shape=[jax.ShapeDtypeStruct(shape, keys.dtype) for shape in (laid, halo, halo)],
        name="pack_edges",
    )(keys, values, *streams, *streams)


def pack_rows_kernel(split, q_ref, g_ref, *refs):
    outs, sems = refs[:-1], refs[-1]
    width = outs[0].shape[1] // 2
    slot = own_slot(split)
    copies = []
    for distance, out in enumerate(outs):
        part = pl.ds(pl.multiple_of((slot ^ distance) * width, HD), width)
        for ref, first in ((q_ref, 0), (g_ref, width)):
            copies.append(
                pltpu.make_async_copy(
                    ref.at[:, part], out.at[:, first : first + width], sems.at[len(copies)]
                )
            )
    for copy in copies:
        copy.start()
    for copy in copies:
        copy.wait()


def pack_rows(queries, grads, slots, split):
    rows, columns = queries.shape
    shape = jax.ShapeDtypeStruct((rows, 2 * columns // slots), queries.dtype)
    return pl.pallas_call(
        functools.partial(pack_rows_kernel, split),
        in_specs=[pl.BlockSpec(memory_space=pltpu.VMEM)] * 2,
        out_specs=[pl.BlockSpec(memory_space=pltpu.HBM)] * slots,
        out_shape=[shape] * slots,
        scratch_shapes=[pltpu.SemaphoreType.DMA((2 * slots,))],
        compiler_params=pltpu.CompilerParams(vmem_limit_bytes=VMEM_PACK),
        name="pack_rows",
    )(queries, grads)


def attention_kernel(pieces, distances, groups, prior, *refs):
    (info_ref, lengths_ref), refs = refs[:2], refs[2:]
    steps = len(distances)
    qg_refs, refs = refs[: steps * groups], refs[steps * groups :]
    piece_refs, refs = refs[:pieces], refs[pieces:]
    prior_refs, refs = refs[: prior * pieces], refs[prior * pieces :]
    out_refs, refs = refs[:steps], refs[steps:]
    term_refs, refs = refs[:pieces], refs[pieces:]
    kv, k_t, v_t, dk_sum, dv_sum, scores, weights, dscores = refs[:8]
    q_rows, q_t, g_rows, g_t, peak8, total8, out_t, dq_t = refs[8:]
    step = pl.program_id(0)
    blocks = k_t.shape[0]
    run = qg_refs[0].shape[0]
    columns = qg_refs[0].shape[1] // 2
    heads = columns // HD
    size = groups * run
    rows = size * heads
    f32 = jnp.float32
    bf16 = jnp.bfloat16
    chunks = [slice(start, min(start + 256, rows)) for start in range(0, rows, 256)]
    ctx = lax.axis_index("ctx")
    own = lax.axis_index("tp") if groups > 1 else 0
    origin = info_ref[0]

    def record_start(position):
        ends = 0
        start = position * 0
        for record in range(lengths_ref.shape[0]):
            ends = ends + lengths_ref[record]
            start = jnp.where(position >= ends, ends, start)
        return start

    def rows_of(b):
        return pl.ds(pl.multiple_of(b * KB, KB), KB)

    def piece_rows(index):
        count = piece_refs[index].shape[1]
        return pl.ds(pl.multiple_of(info_ref[1 + index], 64), count)

    @pl.when(step == 0)
    def _():
        filled = sum(ref.shape[1] for ref in piece_refs)
        if filled < kv.shape[0]:
            kv[filled:] = jnp.zeros((kv.shape[0] - filled, 2 * HD), bf16)
        for index in range(pieces):
            kv[piece_rows(index), :HD] = piece_refs[index][0]
            kv[piece_rows(index), HD:] = piece_refs[index][1]
        dk_sum[...] = jnp.zeros(dk_sum.shape, f32)
        dv_sum[...] = jnp.zeros(dv_sum.shape, f32)

        def prepare(b, carry):
            k_t[b] = kv[rows_of(b), :HD].T
            v_t[b] = kv[rows_of(b), HD:].T
            return carry

        lax.fori_loop(0, blocks, prepare, 0)

    for which in range(steps):

        @pl.when(step == which)
        def _():
            for a in range(groups):
                ref = qg_refs[which * groups + a]
                for h in range(heads):
                    part = slice(h * size + a * run, h * size + (a + 1) * run)
                    q_rows[part] = ref[:, h * HD : (h + 1) * HD]
                    g_rows[part] = ref[:, columns + h * HD : columns + (h + 1) * HD]

    q_t[...] = q_rows[...].T
    g_t[...] = g_rows[...].T
    peak8[...] = jnp.full((8, rows), NEG, f32)
    total8[...] = jnp.zeros((8, rows), f32)
    out_t[...] = jnp.zeros((HD, rows), f32)
    dq_t[...] = jnp.zeros((HD, rows), f32)

    distance = distances[0]
    for which in range(1, steps):
        distance = jnp.where(step == which, distances[which], distance)
    q_first = (ctx ^ distance) * size
    low_first = record_start(q_first)
    low_last = record_start(q_first + (size - 1))
    token = lax.broadcasted_iota(jnp.int32, (1, rows), 1) % size
    if groups > 1:
        token = ((token // run) ^ own) * run + token % run
    pos = q_first + token
    low = record_start(pos)
    first = (low_first - origin) // KB
    last = (q_first + (size - 1) - origin) // KB + 1

    def fold(values, combine):
        result = values[0:8]
        for start in range(8, values.shape[0], 8):
            result = combine(result, values[start : start + 8])
        return result

    def score_pass(b, carry):
        base = origin + b * KB
        whole = (base + (KB - 1) <= q_first) & (base >= low_last)

        @pl.when(whole)
        def _():
            for part in chunks:
                s = jnp.dot(kv[rows_of(b), :HD], q_t[:, part], preferred_element_type=f32)
                scores[b - first, :, part] = s
                peak8[:, part] = jnp.maximum(peak8[:, part], fold(s, jnp.maximum))

        @pl.when(jnp.logical_not(whole))
        def _():
            for part in chunks:
                s = jnp.dot(kv[rows_of(b), :HD], q_t[:, part], preferred_element_type=f32)
                key_pos = base + lax.broadcasted_iota(jnp.int32, s.shape, 0)
                allowed = (key_pos <= pos[:, part]) & (key_pos >= low[:, part])
                s = jnp.where(allowed, s, NEG)
                scores[b - first, :, part] = s
                peak8[:, part] = jnp.maximum(peak8[:, part], fold(s, jnp.maximum))

        return carry

    lax.fori_loop(first, last, score_pass, 0)
    peak = jnp.max(peak8[...], axis=0, keepdims=True) * TO_EXP2

    def weight_pass(b, carry):
        for part in chunks:
            w = jnp.exp2(scores[b - first, :, part] * TO_EXP2 - peak[:, part])
            total8[:, part] += fold(w, jnp.add)
            w_b = w.astype(bf16)
            weights[b - first, :, part] = w_b
            out_t[:, part] += jnp.dot(v_t[b], w_b, preferred_element_type=f32)
        return carry

    lax.fori_loop(first, last, weight_pass, 0)
    inverse = 1.0 / jnp.sum(total8[...], axis=0, keepdims=True)
    out_b = (out_t[...] * inverse).astype(bf16)
    g_wide = g_t[...].astype(f32)
    delta = jnp.sum(g_wide * out_b.astype(f32), axis=0, keepdims=True) * inverse
    g_scaled = (g_wide * inverse).astype(bf16)
    g_t[...] = g_scaled
    g_rows[...] = g_scaled.T

    def give(wide, first):
        for which in range(steps):

            @pl.when(step == which)
            def _():
                for a in range(groups):
                    to = pl.ds(pl.multiple_of((own ^ a) * run, 16), run)
                    for h in range(heads):
                        start = h * size + a * run
                        out_refs[which][to, first + h * HD : first + (h + 1) * HD] = wide[
                            start : start + run
                        ]

    give(out_b.T, 0)

    def grad_pass(b, carry):
        for part in chunks:
            dp = jnp.dot(kv[rows_of(b), HD:], g_t[:, part], preferred_element_type=f32)
            w = weights[b - first, :, part].astype(f32)
            dscores[:, part] = (w * (dp - delta[:, part])).astype(bf16)
        dv_sum[rows_of(b)] += jnp.dot(weights[b - first], g_rows[...], preferred_element_type=f32)
        dk_sum[rows_of(b)] += jnp.dot(dscores[...], q_rows[...], preferred_element_type=f32)
        dq_t[...] += jnp.dot(k_t[b], dscores[...], preferred_element_type=f32)
        return carry

    lax.fori_loop(first, last, grad_pass, 0)
    give((dq_t[...] * SCALE).astype(bf16).T, heads * HD)

    @pl.when(step == steps - 1)
    def _():
        for index in range(pieces):
            dk = dk_sum[piece_rows(index)] * SCALE
            dv = dv_sum[piece_rows(index)]
            if prior:
                dk = dk + prior_refs[index][0].astype(f32)
                dv = dv + prior_refs[index][1].astype(f32)
            term_refs[index][0] = dk.astype(bf16)
            term_refs[index][1] = dv.astype(bf16)


def attention(qg_pieces, kv_pieces, info, lengths, distances, most, prior=()):
    run, columns = qg_pieces[0].shape
    steps = len(distances)
    groups = len(qg_pieces) // steps
    size = groups * run
    heads = columns // (2 * HD)
    rows = size * heads
    pieces = len(kv_pieces)
    keys = -(-sum(part.shape[1] for part in kv_pieces) // KB) * KB
    blocks = keys // KB
    live = min(blocks, (most + size - 3) // KB + 2)
    bf16 = jnp.bfloat16
    f32 = jnp.float32

    def still(shape):
        return pl.BlockSpec(shape, lambda i, *_: (0,) * len(shape))

    kv_specs = [still(part.shape) for part in kv_pieces]
    given = (size, columns)
    pairs = size * steps * heads * keys
    results = pl.pallas_call(
        functools.partial(attention_kernel, pieces, distances, groups, 1 if prior else 0),
        grid_spec=pltpu.PrefetchScalarGridSpec(
            num_scalar_prefetch=2,
            grid=(steps,),
            in_specs=[still((run, columns))] * len(qg_pieces)
            + kv_specs
            + (kv_specs if prior else []),
            out_specs=[still(given)] * steps + kv_specs,
            scratch_shapes=[
                pltpu.VMEM((keys, 2 * HD), bf16),
                pltpu.VMEM((blocks, HD, KB), bf16),
                pltpu.VMEM((blocks, HD, KB), bf16),
                pltpu.VMEM((keys, HD), f32),
                pltpu.VMEM((keys, HD), f32),
                pltpu.VMEM((live, KB, rows), f32),
                pltpu.VMEM((live, KB, rows), bf16),
                pltpu.VMEM((KB, rows), bf16),
                pltpu.VMEM((rows, HD), bf16),
                pltpu.VMEM((HD, rows), bf16),
                pltpu.VMEM((rows, HD), bf16),
                pltpu.VMEM((HD, rows), bf16),
                pltpu.VMEM((8, rows), f32),
                pltpu.VMEM((8, rows), f32),
                pltpu.VMEM((HD, rows), f32),
                pltpu.VMEM((HD, rows), f32),
            ],
        ),
        out_shape=[jax.ShapeDtypeStruct(given, bf16)] * steps
        + [jax.ShapeDtypeStruct(part.shape, bf16) for part in kv_pieces],
        compiler_params=pltpu.CompilerParams(vmem_limit_bytes=VMEM),
        cost_estimate=pl.CostEstimate(
            flops=48 * HD * pairs, bytes_accessed=32 * rows * HD * steps, transcendentals=pairs
        ),
        name="attention",
    )(info, lengths, *qg_pieces, *kv_pieces, *prior)
    return results[:steps], results[steps:]


def settle_kernel(split, *refs):
    piece_refs, (out_ref, dq_ref) = refs[:split], refs[split:]
    width = piece_refs[0].shape[1] // 2
    core = lax.axis_index("ctx") % split
    for distance in range(split):
        to = pl.ds(pl.multiple_of((core ^ distance) * width, HD), width)
        out_ref[:, to] = piece_refs[distance][:, :width]
        dq_ref[:, to] = piece_refs[distance][:, width:]


def settle(parts):
    split = len(parts)
    rows, width = parts[0].shape
    shape = jax.ShapeDtypeStruct((rows, width * split // 2), parts[0].dtype)
    return pl.pallas_call(
        functools.partial(settle_kernel, split),
        out_shape=[shape] * 2,
        compiler_params=pltpu.CompilerParams(vmem_limit_bytes=VMEM),
        name="settle",
    )(*parts)


def body(
    record_lengths,
    query_heads,
    key_heads,
    value_heads,
    out_grad,
    gate_input,
    key_input,
    value_input,
    hyena_grad,
    short_filter,
    long_filter,
):
    ctx = lax.axis_size("ctx")
    tp = lax.axis_size("tp")
    own_ctx = lax.axis_index("ctx")
    piece = query_heads.shape[0]
    tokens = piece * tp
    window = tokens * ctx
    most = window // 2 + 192
    split = PLANE if (KVH // tp) % PLANE == 0 else 1
    slots = tp * split
    kv_local = KVH // slots
    assert kv_local == 1 and tokens % 192 == 0
    unit = tokens * split
    lanes = PLANE // split
    plane = unit * lanes
    reach = (most - 1) // plane
    tail = -(-(most - 1 - reach * plane) // 192) * 192
    core = own_ctx % split
    lane = own_ctx // split % lanes
    level = own_ctx // PLANE
    f32 = jnp.float32
    bf16 = jnp.bfloat16

    members = [
        [t * ctx + n * split + c for t in range(tp) for c in range(split)]
        for n in range(ctx // split)
    ]

    def share(laid):
        return lax.all_to_all(
            laid, ("tp", "ctx"), 0, 0, axis_index_groups=members, tiled=True
        )

    permute = functools.partial(lax.ppermute, axis_name="ctx")

    def across(values, distance):
        return permute(values, perm=[(i, i ^ (distance * split)) for i in range(ctx)])

    def up(values):
        return permute(values, perm=[(i, i + PLANE) for i in range(ctx - PLANE)])

    def down(values):
        return permute(values, perm=[(i + PLANE, i) for i in range(ctx - PLANE)])

    def swap(values, distance):
        return permute(values, perm=[(i, i ^ distance) for i in range(ctx)])

    far = (reach + 1) * PLANE - (lanes - 1) * split
    far_pairs = [
        (i, i + far) for i in range(ctx - far) if i // split % lanes == lanes - 1
    ]

    streams = (gate_input, key_input, value_input, hyena_grad)
    laid_kv, inner, outer = pack_edges(key_heads, value_heads, streams, slots)
    inner = permute(inner, perm=[(i, i ^ 1) for i in range(ctx)])
    outer = permute(
        outer, perm=[(i, (i + 1 if i % 2 else i - 1)) for i in range(1, ctx - 1)]
    )

    kv = share(laid_kv)
    if piece % 32:
        cut = [part.reshape(piece, slots, -1) for part in (query_heads, out_grad)]
        laid = jnp.concatenate(cut, axis=2).transpose(1, 0, 2)
        qg = share(laid).reshape(tp, split, piece, -1).transpose(1, 0, 2, 3)
        qg = list(qg.reshape(split, tokens, -1))
    else:
        laid_kv, query_heads = lax.optimization_barrier((laid_kv, query_heads))
        qg = list(pack_rows(query_heads, out_grad, slots, split))

    def exchange(which):
        for distance in which:
            far_t, far_c = distance // split, distance % split
            perm = [
                (i * tp + t, (i ^ far_c) * tp + (t ^ far_t))
                for t in range(tp)
                for i in range(ctx)
            ]
            qg[distance] = lax.ppermute(qg[distance], ("ctx", "tp"), perm)

    calls = [(split - 1, 0), (split // 2, split // 2 - 1)] if split > 1 else [(0,)]

    def rows_for(call):
        return [a * split + c for c in calls[call] for a in range(tp)]

    if piece % 32 == 0:
        first = [d for d in rows_for(0) if d]
    kv, inner, outer, qg[0] = lax.optimization_barrier((kv, inner, outer, qg[0]))
    own_kv = kv.reshape(tp, split, 2, piece, kv_local * HD)
    own_kv = own_kv.transpose(2, 1, 0, 3, 4).reshape(2, unit, kv_local * HD)

    filters = (short_filter, long_filter)
    columns = [own_kv]
    if piece % 32 == 0:
        own_kv, *held = lax.optimization_barrier((own_kv,) + tuple(qg[d] for d in first))
        columns = [own_kv]
        for distance, value in zip(first, held):
            qg[distance] = value
        exchange(first)
    for hop in range(reach):
        coming = up(columns[-1])
        if hop == reach - 1:
            inner, columns[-1] = lax.optimization_barrier((inner, columns[-1]))
            hyena_outs = hyena(streams, inner, outer, *filters, 0, 4)
            coming, first_out = lax.optimization_barrier((coming, hyena_outs[0]))
            hyena_outs = [first_out] + list(hyena_outs[1:])
        columns.append(coming)
    tail_kv = own_kv[:, unit - tail :]
    tail_kv, columns[1] = lax.optimization_barrier((tail_kv, columns[1]))
    tail_kv = permute(tail_kv, perm=far_pairs)
    pieces = [tail_kv]
    places = [jnp.int32(0)]
    for back in range(reach + 1):
        for distance in range(lanes):
            held = columns[back]
            pieces.append(held if distance == 0 else across(held, distance))
            places.append(tail + (reach - back) * plane + (lane ^ distance) * unit)
    origin = (level - reach) * plane - tail
    info = jnp.stack([origin] + places).astype(jnp.int32)

    owners = [None] * split
    terms = ()
    arrived = None
    for call, distances in enumerate(calls):
        if call:
            exchange(rows_for(call))
        held = [qg[d] for d in rows_for(call)] if piece % 32 == 0 else qg
        outs, terms = attention(held, pieces, info, record_lengths, distances, most, terms)
        if arrived is not None:
            at = 1 + reach * lanes
            terms = list(terms)
            arrived, terms[at] = lax.optimization_barrier((arrived, terms[at]))
            owners[calls[0][0]] = arrived
        for distance, value in zip(distances, outs):
            owners[distance] = swap(value, distance) if distance else value
        if call == 0 and split > 1:
            arrived = owners[distances[0]]
    attn_out, grad_query = settle(owners)

    def plane_sum(back):
        at = 1 + back * lanes
        total = terms[at].astype(f32)
        for distance in range(1, lanes):
            total = total + across(terms[at + distance], distance).astype(f32)
        return total

    tail_term = permute(terms[0], perm=[(j, i) for i, j in far_pairs])
    running = plane_sum(reach).astype(bf16)
    for back in range(reach - 1, -1, -1):
        coming = down(running)
        if back == reach - 1:
            inner, running = lax.optimization_barrier((inner, running))
            hyena_outs = hyena(streams, inner, outer, *filters, 4, 4, hyena_outs)
            coming, first_out = lax.optimization_barrier((coming, hyena_outs[0]))
            hyena_outs = [first_out] + list(hyena_outs[1:])
        running = plane_sum(back) + coming.astype(f32)
        if back:
            running = running.astype(bf16)
    running, attn_out = lax.optimization_barrier((running, attn_out))
    owned = jnp.concatenate(
        [running[:, : unit - tail], running[:, unit - tail :] + tail_term.astype(f32)], axis=1
    ).astype(bf16)

    parts = []
    for distance in range(split):
        held = lax.dynamic_slice_in_dim(owned, (core ^ distance) * tokens, tokens, 1)
        parts.append(swap(held, distance) if distance else held)
    bit = 1
    while bit < split:
        parts = [
            jnp.where(core & bit != 0, parts[index ^ bit], parts[index]) for index in range(split)
        ]
        bit = 2 * bit
    grads = jnp.concatenate(parts, axis=2)
    return (attn_out, grad_query, grads[0], grads[1]) + tuple(hyena_outs)


def solution(mesh):
    rows = P(("ctx", "tp"), None)
    both = P("ctx", "tp")
    return jax.shard_map(
        body,
        mesh=mesh,
        in_specs=(P(), rows, rows, rows, rows, both, both, both, both)
        + (P(None, None, "tp"), P(None, "tp")),
        out_specs=(both,) * 8,
        check_vma=False,
    )
```

profile of v0, /device:TPU:0, one launch (start us, length us, event | category | flops | bytes accessed | tf_op | source)
XLA Modules:
  0.0 145.1 jit_solution(2672040276474007310)
XLA Ops:
  0.6 2.5 %pack_edges.1 = (bf16[8,2,96,128]{3,2,1,0:T(8,128)(2,1)}, bf16[32,4096]{1,0:T(8,128)(2,1)}, bf16[32,4096]{1,0:T(8,128)(2,1)}) custom-call(bf16[96,1024]{1,0:T(8,128)(2,1)} %k_ref.1, bf16[96,1024]{1,0:T(8,128)(2,1)} %v_ref.1, bf16[192,4096]{1,0:T(8,128)(2,1)} %gate_ref.3, bf16[192,4096]{1,0:T(8,128)(2,1)} %key_ref.3, bf16[192,4096]{1,0:T(8,128)(2,1)} %value_ref.3, ...), custom_call_target="tpu_custom_call" | custom-call | tf_op jit(solution)/shard_map/pack_edges/pallas_call | solution.py:189
  3.1 5.2 %all-to-all-start = ((bf16[8,2,96,128]{3,2,1,0:T(8,128)(2,1)}), bf16[8,2,96,128]{3,2,1,0:T(8,128)(2,1)}, u32[]{:S(2)}, u32[]{:S(2)}) async-start(bf16[8,2,96,128]{3,2,1,0:T(8,128)(2,1)} %get-tuple-element.63), calls=%async_computation | async-start | bytes 786432 | tf_op jit(solution)/shard_map/all_to_all | solution.py:537
  8.8 1.5 %collective-permute-start.5 = (bf16[32,4096]{1,0:T(8,128)(2,1)}, bf16[32,4096]{1,0:T(8,128)(2,1)}, u32[]{:S(2)}, u32[]{:S(2)}) collective-permute-start(bf16[32,4096]{1,0:T(8,128)(2,1)} %get-tuple-element.70), channel_id=1, source_target_pairs={{2,4},{4,2},{6,8},{8,6},{10,12},{12,10},{14,16},{16,14},{18,20},{2... | collective-permute-start | bytes 786440 | tf_op jit(solution)/shard_map/ppermute | solution.py:563
  10.3 3.7 %pack_rows.1 = (bf16[96,2048]{1,0:T(8,128)(2,1)}, bf16[96,2048]{1,0:T(8,128)(2,1)}, bf16[96,2048]{1,0:T(8,128)(2,1)}, bf16[96,2048]{1,0:T(8,128)(2,1)}, bf16[96,...) custom-call(bf16[96,8192]{1,0:T(8,128)(2,1)} %q_ref, ...), custom_call_target="tpu_custom_call" | custom-call | tf_op jit(solution)/shard_map/pack_rows/pallas_call | solution.py:225
  14.0 2.7 %all-to-all-done = bf16[8,2,96,128]{3,2,1,0:T(8,128)(2,1)} async-done(((bf16[8,2,96,128]{3,2,1,0:T(8,128)(2,1)}), bf16[8,2,96,128]{3,2,1,0:T(8,128)(2,1)}, u32[]{:S(2)}, u32[]{:S(2)}) %all-to-all-start) | async-done | bytes 393248 | tf_op jit(solution)/shard_map/all_to_all | solution.py:537
  16.7 1.0 copy.23
  17.8 6.6 %collective-permute-start.6 = (bf16[2,768,128]{2,1,0:T(8,128)(2,1)S(1)}, bf16[2,768,128]{2,1,0:T(8,128)(2,1)S(1)}, u32[]{:S(2)}, u32[]{:S(2)}) collective-permute-start(bf16[2,768,128]{2,1,0:T(8,128)(2,1)S(1)} %bitcast.9), channel_id=1, source_target_pairs={{0,8},{2,10},{4,12},{6,14},{8,16},{10,18},{12,20},{14,22},{16,24},... | collective-permute-start | bytes 1179656 | tf_op jit(solution)/shard_map/ppermute | solution.py:547
  25.7 1.7 %collective-permute-start.9 = (bf16[96,2048]{1,0:T(8,128)(2,1)}, bf16[96,2048]{1,0:T(8,128)(2,1)S(1)}, u32[]{:S(2)}, u32[]{:S(2)}) collective-permute-start(bf16[96,2048]{1,0:T(8,128)(2,1)} %get-tuple-element.85), channel_id=1, source_target_pairs={{0,6},{2,4},{4,2},{6,0},{8,14},{10,12},{12,10},{14,8},{16,22},{18,... | collective-permute-start | bytes 1179656 | tf_op jit(solution)/shard_map/ppermute | solution.py:585
  27.5 5.7 %collective-permute-done.6.refs_8_ = bf16[2,768,128]{2,1,0:T(8,128)(2,1)S(1)} collective-permute-done((bf16[2,768,128]{2,1,0:T(8,128)(2,1)S(1)}, bf16[2,768,128]{2,1,0:T(8,128)(2,1)S(1)}, u32[]{:S(2)}, u32[]{:S(2)}) %collective-permute-start.6) | collective-permute-done | bytes 393248 | tf_op jit(solution)/shard_map/ppermute | solution.py:547
  33.1 6.4 %collective-permute-start.7 = (bf16[2,192,128]{2,1,0:T(8,128)(2,1)S(1)}, bf16[2,192,128]{2,1,0:T(8,128)(2,1)S(1)}, u32[]{:S(2)}, u32[]{:S(2)}) collective-permute-start(bf16[2,192,128]{2,1,0:T(8,128)(2,1)S(1)} %slice.16), channel_id=1, source_target_pairs={{0,24},{2,26},{4,28},{6,30},{1,25},{3,27},{5,29},{7,31}} | collective-permute-start | bytes 294920 | tf_op jit(solution)/shard_map/ppermute | solution.py:616
  39.5 1.3 collective-permute-start.8
  40.9 1.4 copy-done.1
  42.3 1.4 copy-done.3
  43.7 0.9 copy-done.11
  44.6 0.9 copy-done.12
  45.6 7.7 %hyena.2 = (bf16[192,4096]{1,0:T(8,128)(2,1)}, bf16[192,4096]{1,0:T(8,128)(2,1)}, bf16[192,4096]{1,0:T(8,128)(2,1)}, bf16[192,4096]{1,0:T(8,128)(2,1)}) custom-call(bf16[192,4096]{1,0:T(8,128)(2,1)S(1)} %copy-done, bf16[192,4096]{1,0:T(8,128)(2,1)S(1)} %copy-done.1, bf16[192,4096]{1,0:T(8,128)(2,1)S(1)} %copy-done.3, bf16[192,4096]{1,0:T(8,128)(2,1)} %grad_ref.3, ...), custom_call_target="tpu_custom_call" | custom-call | flops 5505024000 | bytes 6291456 | tf_op jit(solution)/shard_map/hyena/pallas_call | solution.py:127
  54.4 1.0 collective-permute-start.2
  55.4 1.6 %collective-permute-start.3 = (bf16[96,2048]{1,0:T(8,128)(2,1)S(1)}, bf16[96,2048]{1,0:T(8,128)(2,1)S(1)}, u32[]{:S(2)}, u32[]{:S(2)}) collective-permute-start(bf16[96,2048]{1,0:T(8,128)(2,1)S(1)} %copy-done.17), channel_id=1, source_target_pairs={{0,3},{2,1},{4,7},{6,5},{8,11},{10,9},{12,15},{14,13},{16,19},{18,... | collective-permute-start | bytes 1179656 | tf_op jit(solution)/shard_map/ppermute | solution.py:585
  57.1 14.6 %attention.2 = (bf16[192,2048]{1,0:T(8,128)(2,1)S(1)}, bf16[192,2048]{1,0:T(8,128)(2,1)S(1)}, bf16[2,192,128]{2,1,0:T(8,128)(2,1)S(1)}, bf16[2,768,128]{2,1,0:T(...) custom-call(s32[5]{0:T(128)S(1)} %stack.10.refs_0_, s32[16]{0:T(128)S(1)} %copy-done.16, ...), custom_call_target="tpu_custom_call" | custom-call | flops 48318382080 | bytes 12582912 | tf_op jit(solution)/shard_map/attention/pallas_call | solution.py:435
  72.3 2.7 %collective-permute-done.3.refs_5_ = bf16[96,2048]{1,0:T(8,128)(2,1)S(1)} collective-permute-done((bf16[96,2048]{1,0:T(8,128)(2,1)S(1)}, bf16[96,2048]{1,0:T(8,128)(2,1)S(1)}, u32[]{:S(2)}, u32[]{:S(2)}) %collective-permute-start.3) | collective-permute-done | bytes 393248 | tf_op jit(solution)/shard_map/ppermute | solution.py:585
  75.0 1.0 copy-done.8
  76.0 15.9 %attention.3 = (bf16[192,2048]{1,0:T(8,128)(2,1)}, bf16[192,2048]{1,0:T(8,128)(2,1)}, bf16[2,192,128]{2,1,0:T(8,128)(2,1)S(1)}, bf16[2,768,128]{2,1,0:T(8,128)(2...) custom-call(s32[5]{0:T(128)S(1)} %stack.10.refs_0_, s32[16]{0:T(128)S(1)} %copy-done.16, ...), custom_call_target="tpu_custom_call" | custom-call | flops 48318382080 | bytes 12582912 | tf_op jit(solution)/shard_map/attention/pallas_call | solution.py:435
  92.7 1.3 collective-permute-start.13
  94.0 7.9 %hyena.3 = (bf16[192,4096]{1,0:T(8,128)(2,1)}, bf16[192,4096]{1,0:T(8,128)(2,1)}, bf16[192,4096]{1,0:T(8,128)(2,1)}, bf16[192,4096]{1,0:T(8,128)(2,1)}) custom-call(bf16[192,4096]{1,0:T(8,128)(2,1)S(1)} %copy-done, bf16[192,4096]{1,0:T(8,128)(2,1)S(1)} %copy-done.2, ...), custom_call_target="tpu_custom_call", output_to_operand_aliasing={{0}: (8, {}), {1}: (9, {}), {2}: (10, {}), {3}: (11, {})} | custom-call | flops 5505024000 | bytes 6291456 | tf_op jit(solution)/shard_map/hyena/pallas_call | solution.py:127
  101.9 20.3 %collective-permute-done.13 = bf16[2,768,128]{2,1,0:T(8,128)(2,1)S(1)} collective-permute-done((bf16[2,768,128]{2,1,0:T(8,128)(2,1)S(1)}, bf16[2,768,128]{2,1,0:T(8,128)(2,1)S(1)}, u32[]{:S(2)}, u32[]{:S(2)}) %collective-permute-start.13) | collective-permute-done | bytes 393248 | tf_op jit(solution)/shard_map/ppermute | solution.py:550
  123.1 1.3 collective-permute-start.14
  124.4 1.3 collective-permute-start.17
  125.7 3.3 %settle.1 = (bf16[192,4096]{1,0:T(8,128)(2,1)}, bf16[192,4096]{1,0:T(8,128)(2,1)}) custom-call(bf16[192,2048]{1,0:T(8,128)(2,1)S(1)} %get-tuple-element.105.refs_0_, bf16[192,2048]{1,0:T(8,128)(2,1)} %collective-permute-done.15.refs_1_, bf16[192,2048]{1,0:T(8,128)(2,1)} %collective-permute-done.16.refs_2_, bf16[192,2048]{1,0:T(8,128)(2,1)S(1)} %copy-done.6), custom_call_target="tpu_custom_call" | custom-call | tf_op jit(solution)/shard_map/settle/pallas_call | solution.py:488
  129.0 7.5 %collective-permute-done.14 = bf16[2,768,128]{2,1,0:T(8,128)(2,1)S(1)} collective-permute-done((bf16[2,768,128]{2,1,0:T(8,128)(2,1)}, bf16[2,768,128]{2,1,0:T(8,128)(2,1)S(1)}, u32[]{:S(2)}, u32[]{:S(2)}) %collective-permute-start.14) | collective-permute-done | bytes 393248 | tf_op jit(solution)/shard_map/ppermute | solution.py:550
  136.6 1.1 collective-permute-done.17
  139.0 1.2 collective-permute-start.20
  140.2 3.1 %collective-permute-done.18 = bf16[2,192,128]{2,1,0:T(8,128)(2,1)S(1)} collective-permute-done((bf16[2,192,128]{2,1,0:T(8,128)(2,1)S(1)}, bf16[2,192,128]{2,1,0:T(8,128)(2,1)S(1)}, u32[]{:S(2)}, u32[]{:S(2)}) %collective-permute-start.18) | collective-permute-done | bytes 98336 | tf_op jit(solution)/shard_map/ppermute | solution.py:553
  (73 shorter events, 8.3 us)
Async XLA Ops:
  3.1 13.6 %all-to-all-start = ((bf16[8,2,96,128]{3,2,1,0:T(8,128)(2,1)}), bf16[8,2,96,128]{3,2,1,0:T(8,128)(2,1)}, u32[]{:S(2)}, u32[]{:S(2)}) async-start(bf16[8,2,96,128]{3,2,1,0:T(8,128)(2,1)} %get-tuple-element.63), calls=%async_computation | async-start | bytes 786432 | tf_op jit(solution)/shard_map/all_to_all | solution.py:537
  8.3 5.7 %collective-permute-start.4 = (bf16[32,4096]{1,0:T(8,128)(2,1)}, bf16[32,4096]{1,0:T(8,128)(2,1)S(1)}, u32[]{:S(2)}, u32[]{:S(2)}) collective-permute-start(bf16[32,4096]{1,0:T(8,128)(2,1)} %get-tuple-element.69), channel_id=1, source_target_pairs={{0,2},{2,0},{4,6},{6,4},{8,10},{10,8},{12,14},{14,12},{16,18},{18,... | collective-permute-start | bytes 786440 | tf_op jit(solution)/shard_map/ppermute | solution.py:562
  8.8 32.1 %copy-start = (bf16[192,4096]{1,0:T(8,128)(2,1)S(1)}, bf16[192,4096]{1,0:T(8,128)(2,1)}, u32[]{:S(2)}) copy-start(bf16[192,4096]{1,0:T(8,128)(2,1)} %gate_ref.3) | copy-start | bytes 4718596
  8.8 32.1 %copy-start.15 = (f32[7,256]{1,0:T(8,128)S(1)}, f32[7,256]{1,0:T(8,128)}, u32[]{:S(2)}) copy-start(f32[7,256]{1,0:T(8,128)} %long_ref.3) | copy-start | bytes 21508
  8.8 5.2 %collective-permute-start.5 = (bf16[32,4096]{1,0:T(8,128)(2,1)}, bf16[32,4096]{1,0:T(8,128)(2,1)}, u32[]{:S(2)}, u32[]{:S(2)}) collective-permute-start(bf16[32,4096]{1,0:T(8,128)(2,1)} %get-tuple-element.70), channel_id=1, source_target_pairs={{2,4},{4,2},{6,8},{8,6},{10,12},{12,10},{14,16},{16,14},{18,20},{2... | collective-permute-start | bytes 786440 | tf_op jit(solution)/shard_map/ppermute | solution.py:563
  17.8 15.4 %collective-permute-start.6 = (bf16[2,768,128]{2,1,0:T(8,128)(2,1)S(1)}, bf16[2,768,128]{2,1,0:T(8,128)(2,1)S(1)}, u32[]{:S(2)}, u32[]{:S(2)}) collective-permute-start(bf16[2,768,128]{2,1,0:T(8,128)(2,1)S(1)} %bitcast.9), channel_id=1, source_target_pairs={{0,8},{2,10},{4,12},{6,14},{8,16},{10,18},{12,20},{14,22},{16,24},... | collective-permute-start | bytes 1179656 | tf_op jit(solution)/shard_map/ppermute | solution.py:547
  24.5 32.6 %copy-start.16 = (s32[16]{0:T(128)S(1)}, s32[16]{0:T(128)}, u32[]{:S(2)}) copy-start(s32[16]{0:T(128)} %refs_1_.5) | copy-start | bytes 196
  24.5 28.9 %collective-permute-start.10 = (bf16[96,2048]{1,0:T(8,128)(2,1)}, bf16[96,2048]{1,0:T(8,128)(2,1)S(1)}, u32[]{:S(2)}, u32[]{:S(2)}) collective-permute-start(bf16[96,2048]{1,0:T(8,128)(2,1)} %get-tuple-element.86), channel_id=1, source_target_pairs={{0,7},{2,5},{4,3},{6,1},{8,15},{10,13},{12,11},{14,9},{16,23},{18,... | collective-permute-start | bytes 1179656 | tf_op jit(solution)/shard_map/ppermute | solution.py:585
  25.2 29.2 %collective-permute-start.11 = (bf16[96,2048]{1,0:T(8,128)(2,1)}, bf16[96,2048]{1,0:T(8,128)(2,1)S(1)}, u32[]{:S(2)}, u32[]{:S(2)}) collective-permute-start(bf16[96,2048]{1,0:T(8,128)(2,1)} %get-tuple-element.88), channel_id=1, source_target_pairs={{0,1},{2,3},{4,5},{6,7},{8,9},{10,11},{12,13},{14,15},{16,17},{18,... | collective-permute-start | bytes 1179656 | tf_op jit(solution)/shard_map/ppermute | solution.py:585
  25.7 29.7 %collective-permute-start.9 = (bf16[96,2048]{1,0:T(8,128)(2,1)}, bf16[96,2048]{1,0:T(8,128)(2,1)S(1)}, u32[]{:S(2)}, u32[]{:S(2)}) collective-permute-start(bf16[96,2048]{1,0:T(8,128)(2,1)} %get-tuple-element.85), channel_id=1, source_target_pairs={{0,6},{2,4},{4,2},{6,0},{8,14},{10,12},{12,10},{14,8},{16,22},{18,... | collective-permute-start | bytes 1179656 | tf_op jit(solution)/shard_map/ppermute | solution.py:585
  33.1 23.9 %copy-start.7 = (bf16[2,768,128]{2,1,0:T(8,128)(2,1)}, bf16[2,768,128]{2,1,0:T(8,128)(2,1)S(1)}, u32[]{:S(2)}) copy-start(bf16[2,768,128]{2,1,0:T(8,128)(2,1)S(1)} %collective-permute-done.6.refs_8_) | copy-start | bytes 1179652
  33.1 23.9 %collective-permute-start.7 = (bf16[2,192,128]{2,1,0:T(8,128)(2,1)S(1)}, bf16[2,192,128]{2,1,0:T(8,128)(2,1)S(1)}, u32[]{:S(2)}, u32[]{:S(2)}) collective-permute-start(bf16[2,192,128]{2,1,0:T(8,128)(2,1)S(1)} %slice.16), channel_id=1, source_target_pairs={{0,24},{2,26},{4,28},{6,30},{1,25},{3,27},{5,29},{7,31}} | collective-permute-start | bytes 294920 | tf_op jit(solution)/shard_map/ppermute | solution.py:616
  39.5 13.8 %collective-permute-start.8 = (bf16[2,768,128]{2,1,0:T(8,128)(2,1)S(1)}, bf16[2,768,128]{2,1,0:T(8,128)(2,1)S(1)}, u32[]{:S(2)}, u32[]{:S(2)}) collective-permute-start(bf16[2,768,128]{2,1,0:T(8,128)(2,1)S(1)} %collective-permute-done.6.refs_8_), channel_id=1, source_target_pairs={{0,8},{2,10},{4,12},{6,14},{8,16},{10,18},{12,20},{14,22},{16,24},... | collective-permute-start | bytes 1179656 | tf_op jit(solution)/shard_map/ppermute | solution.py:547
  45.6 9.8 %copy-start.17 = (bf16[96,2048]{1,0:T(8,128)(2,1)S(1)}, bf16[96,2048]{1,0:T(8,128)(2,1)}, u32[]{:S(2)}) copy-start(bf16[96,2048]{1,0:T(8,128)(2,1)} %get-tuple-element.68) | copy-start | bytes 1179652
  45.6 11.5 %copy-start.9 = (bf16[96,2048]{1,0:T(8,128)(2,1)S(1)}, bf16[96,2048]{1,0:T(8,128)(2,1)}, u32[]{:S(2)}) copy-start(bf16[96,2048]{1,0:T(8,128)(2,1)} %get-tuple-element.87.refs_4_) | copy-start | bytes 1179652
  53.3 18.4 %collective-permute-start = (bf16[96,2048]{1,0:T(8,128)(2,1)S(1)}, bf16[96,2048]{1,0:T(8,128)(2,1)S(1)}, u32[]{:S(2)}, u32[]{:S(2)}) collective-permute-start(bf16[96,2048]{1,0:T(8,128)(2,1)S(1)} %copy-done.20), channel_id=1, source_target_pairs={{0,4},{2,6},{4,0},{6,2},{8,12},{10,14},{12,8},{14,10},{16,20},{18,... | collective-permute-start | bytes 1179656 | tf_op jit(solution)/shard_map/ppermute | solution.py:585
  53.4 18.8 %collective-permute-start.1 = (bf16[96,2048]{1,0:T(8,128)(2,1)S(1)}, bf16[96,2048]{1,0:T(8,128)(2,1)S(1)}, u32[]{:S(2)}, u32[]{:S(2)}) collective-permute-start(bf16[96,2048]{1,0:T(8,128)(2,1)S(1)} %copy-done.19), channel_id=1, source_target_pairs={{0,5},{2,7},{4,1},{6,3},{8,13},{10,15},{12,9},{14,11},{16,21},{18,... | collective-permute-start | bytes 1179656 | tf_op jit(solution)/shard_map/ppermute | solution.py:585
  54.4 17.9 %collective-permute-start.2 = (bf16[96,2048]{1,0:T(8,128)(2,1)S(1)}, bf16[96,2048]{1,0:T(8,128)(2,1)S(1)}, u32[]{:S(2)}, u32[]{:S(2)}) collective-permute-start(bf16[96,2048]{1,0:T(8,128)(2,1)S(1)} %copy-done.18), channel_id=1, source_target_pairs={{0,2},{2,0},{4,6},{6,4},{8,10},{10,8},{12,14},{14,12},{16,18},{18,... | collective-permute-start | bytes 1179656 | tf_op jit(solution)/shard_map/ppermute | solution.py:585
  55.4 19.6 %collective-permute-start.3 = (bf16[96,2048]{1,0:T(8,128)(2,1)S(1)}, bf16[96,2048]{1,0:T(8,128)(2,1)S(1)}, u32[]{:S(2)}, u32[]{:S(2)}) collective-permute-start(bf16[96,2048]{1,0:T(8,128)(2,1)S(1)} %copy-done.17), channel_id=1, source_target_pairs={{0,3},{2,1},{4,7},{6,5},{8,11},{10,9},{12,15},{14,13},{16,19},{18,... | collective-permute-start | bytes 1179656 | tf_op jit(solution)/shard_map/ppermute | solution.py:585
  71.7 21.0 %collective-permute-start.12 = (bf16[192,2048]{1,0:T(8,128)(2,1)S(1)}, bf16[192,2048]{1,0:T(8,128)(2,1)S(1)}, u32[]{:S(2)}, u32[]{:S(2)}) collective-permute-start(bf16[192,2048]{1,0:T(8,128)(2,1)S(1)} %get-tuple-element.95), channel_id=1, source_target_pairs={{0,6},{2,4},{4,2},{6,0},{8,14},{10,12},{12,10},{14,8},{16,22},{18,... | collective-permute-start | bytes 2359304 | tf_op jit(solution)/shard_map/ppermute | solution.py:553
  76.0 18.0 %copy-start.2 = (bf16[192,4096]{1,0:T(8,128)(2,1)S(1)}, bf16[192,4096]{1,0:T(8,128)(2,1)}, u32[]{:S(2)}) copy-start(bf16[192,4096]{1,0:T(8,128)(2,1)} %key_ref.3) | copy-start | bytes 4718596
  76.0 18.0 %copy-start.4 = (bf16[192,4096]{1,0:T(8,128)(2,1)S(1)}, bf16[192,4096]{1,0:T(8,128)(2,1)}, u32[]{:S(2)}) copy-start(bf16[192,4096]{1,0:T(8,128)(2,1)} %value_ref.3) | copy-start | bytes 4718596
  76.0 18.0 %copy-start.13 = (f32[3,3,4096]{2,1,0:T(4,128)S(1)}, f32[3,3,4096]{2,1,0:T(4,128)}, u32[]{:S(2)}) copy-start(f32[3,3,4096]{2,1,0:T(4,128)} %short_ref.3) | copy-start | bytes 442372
  91.9 10.0 %copy-start.14 = (bf16[2,192,128]{2,1,0:T(8,128)(2,1)}, bf16[2,192,128]{2,1,0:T(8,128)(2,1)S(1)}, u32[]{:S(2)}) copy-start(bf16[2,192,128]{2,1,0:T(8,128)(2,1)S(1)} %get-tuple-element.113) | copy-start | bytes 294916
  91.9 33.8 %collective-permute-start.15 = (bf16[192,2048]{1,0:T(8,128)(2,1)}, bf16[192,2048]{1,0:T(8,128)(2,1)}, u32[]{:S(2)}, u32[]{:S(2)}) collective-permute-start(bf16[192,2048]{1,0:T(8,128)(2,1)} %get-tuple-element.106), channel_id=1, source_target_pairs={{0,2},{2,0},{4,6},{6,4},{8,10},{10,8},{12,14},{14,12},{16,18},{18,... | collective-permute-start | bytes 2359304 | tf_op jit(solution)/shard_map/ppermute | solution.py:553
  92.2 33.5 %collective-permute-start.16 = (bf16[192,2048]{1,0:T(8,128)(2,1)}, bf16[192,2048]{1,0:T(8,128)(2,1)}, u32[]{:S(2)}, u32[]{:S(2)}) collective-permute-start(bf16[192,2048]{1,0:T(8,128)(2,1)} %get-tuple-element.107), channel_id=1, source_target_pairs={{0,4},{2,6},{4,0},{6,2},{8,12},{10,14},{12,8},{14,10},{16,20},{18,... | collective-permute-start | bytes 2359304 | tf_op jit(solution)/shard_map/ppermute | solution.py:553
  92.7 29.6 %collective-permute-start.13 = (bf16[2,768,128]{2,1,0:T(8,128)(2,1)S(1)}, bf16[2,768,128]{2,1,0:T(8,128)(2,1)S(1)}, u32[]{:S(2)}, u32[]{:S(2)}) collective-permute-start(bf16[2,768,128]{2,1,0:T(8,128)(2,1)S(1)} %get-tuple-element.97), channel_id=1, source_target_pairs={{8,0},{10,2},{12,4},{14,6},{16,8},{18,10},{20,12},{22,14},{24,16},... | collective-permute-start | bytes 1179656 | tf_op jit(solution)/shard_map/ppermute | solution.py:550
  123.1 13.4 %collective-permute-start.14 = (bf16[2,768,128]{2,1,0:T(8,128)(2,1)}, bf16[2,768,128]{2,1,0:T(8,128)(2,1)S(1)}, u32[]{:S(2)}, u32[]{:S(2)}) collective-permute-start(bf16[2,768,128]{2,1,0:T(8,128)(2,1)} %add_convert_fusion), channel_id=1, source_target_pairs={{8,0},{10,2},{12,4},{14,6},{16,8},{18,10},{20,12},{22,14},{24,16},... | collective-permute-start | bytes 1179656 | tf_op jit(solution)/shard_map/ppermute | solution.py:550
  124.4 13.3 %collective-permute-start.17 = (bf16[2,192,128]{2,1,0:T(8,128)(2,1)}, bf16[2,192,128]{2,1,0:T(8,128)(2,1)S(1)}, u32[]{:S(2)}, u32[]{:S(2)}) collective-permute-start(bf16[2,192,128]{2,1,0:T(8,128)(2,1)} %copy-done.14), channel_id=1, source_target_pairs={{24,0},{26,2},{28,4},{30,6},{25,1},{27,3},{29,5},{31,7}} | collective-permute-start | bytes 294920 | tf_op jit(solution)/shard_map/ppermute | solution.py:653
  138.3 5.0 %collective-permute-start.18 = (bf16[2,192,128]{2,1,0:T(8,128)(2,1)S(1)}, bf16[2,192,128]{2,1,0:T(8,128)(2,1)S(1)}, u32[]{:S(2)}, u32[]{:S(2)}) collective-permute-start(bf16[2,192,128]{2,1,0:T(8,128)(2,1)S(1)} %get-tuple-element.126), channel_id=1, source_target_pairs={{0,6},{2,4},{4,2},{6,0},{8,14},{10,12},{12,10},{14,8},{16,22},{18,... | collective-permute-start | bytes 294920 | tf_op jit(solution)/shard_map/ppermute | solution.py:553
  138.3 5.7 %collective-permute-start.19 = (bf16[2,192,128]{2,1,0:T(8,128)(2,1)S(1)}, bf16[2,192,128]{2,1,0:T(8,128)(2,1)S(1)}, u32[]{:S(2)}, u32[]{:S(2)}) collective-permute-start(bf16[2,192,128]{2,1,0:T(8,128)(2,1)S(1)} %get-tuple-element.127), channel_id=1, source_target_pairs={{0,4},{2,6},{4,0},{6,2},{8,12},{10,14},{12,8},{14,10},{16,20},{18,... | collective-permute-start | bytes 294920 | tf_op jit(solution)/shard_map/ppermute | solution.py:553
  139.0 5.0 %collective-permute-start.20 = (bf16[2,192,128]{2,1,0:T(8,128)(2,1)S(1)}, bf16[2,192,128]{2,1,0:T(8,128)(2,1)S(1)}, u32[]{:S(2)}, u32[]{:S(2)}) collective-permute-start(bf16[2,192,128]{2,1,0:T(8,128)(2,1)S(1)} %get-tuple-element.125), channel_id=1, source_target_pairs={{0,2},{2,0},{4,6},{6,4},{8,10},{10,8},{12,14},{14,12},{16,18},{18,... | collective-permute-start | bytes 294920 | tf_op jit(solution)/shard_map/ppermute | solution.py:553
  (11 other events, 46.6 us)
where the time goes:
time: 145 us
  Pallas kernels  55.5 us (38%)
  waiting for transfers between devices  44.4 us (31%)
  starting transfers between devices  34.8 us (24%)
  local copies, waits for them, and re-layouts  7.67 us (5%)
  other arithmetic  1.77 us (1%)
    pallas_call x2, Pallas kernels, attention(): pl.pallas_call(functools.partial(attention_kernel, pieces, distances, gro...  30.5 us
    ppermute x2, waiting for transfers between devices, down(): return permute(values, perm=[(i + PLANE, i) for i in range(ctx - PLANE)])  27.9 us
    pallas_call x2, Pallas kernels, hyena(): pl.pallas_call(functools.partial(hyena_kernel, first * width), grid=(step...  15.6 us
    ppermute x2, starting transfers between devices, up(): return permute(values, perm=[(i, i + PLANE) for i in range(ctx - PLANE)])  7.91 us
    ppermute x7, starting transfers between devices, exchange(): qg[distance] = lax.ppermute(qg[distance], ('ctx', 'tp'), perm)  6.66 us
    ppermute x1, starting transfers between devices, body(): tail_kv = permute(tail_kv, perm=far_pairs)  6.4 us
    unnamed x42, local copies, waits for them, and re-layouts  5.75 us
    ppermute x2, waiting for transfers between devices, up(): return permute(values, perm=[(i, i + PLANE) for i in range(ctx - PLANE)])  5.65 us
  transfers between devices with their start and end apart: 22, of which 9 were waited for; matrix products, arithmetic and copies ran while one was open for 1% of the time, Pallas kernels for 37%

commit v1 on v0

--- a/solution.py
+++ b/solution.py
@@ -143,7 +143,7 @@
         input_output_aliases={8 + i: i for i in range(len(filled))},
         compiler_params=pltpu.CompilerParams(vmem_limit_bytes=VMEM),
         cost_estimate=pl.CostEstimate(
-            flops=14000 * tokens * own, bytes_accessed=16 * tokens * own, transcendentals=0
+            flops=(14000 if filled else 56000) * tokens * own, bytes_accessed=16 * tokens * own, transcendentals=0
         ),
         name="hyena",
     )(*streams, inner, outer, short_filter, long_filter, *filled)
@@ -153,15 +153,15 @@
     return lax.axis_index("tp") * split + lax.axis_index("ctx") % split
 
 
-def pack_edges_kernel(k_ref, v_ref, *refs):
-    streams = (len(refs) - 3) // 2
+def pack_edges_kernel(streams, split, k_ref, v_ref, *refs):
     first_refs, last_refs = refs[:streams], refs[streams : 2 * streams]
-    kv_ref, inner_ref, outer_ref = refs[2 * streams :]
-    width = kv_ref.shape[3]
-    for slot in range(kv_ref.shape[0]):
-        part = slice(slot * width, (slot + 1) * width)
-        kv_ref[slot, 0] = k_ref[:, part]
-        kv_ref[slot, 1] = v_ref[:, part]
+    kv_refs, (inner_ref, outer_ref) = refs[2 * streams : -2], refs[-2:]
+    width = kv_refs[0].shape[2]
+    own = own_slot(split) if split > 1 else 0
+    for distance, ref in enumerate(kv_refs):
+        part = pl.ds(pl.multiple_of((own ^ distance) * width, HD), width)
+        ref[0] = k_ref[:, part]
+        ref[1] = v_ref[:, part]
     f32 = jnp.float32
     odd = lax.axis_index("ctx") % 2
 
@@ -176,7 +176,7 @@
         outer_ref[rows] = jnp.where(odd == 1, tail, head).astype(outer_ref.dtype)
 
 
-def pack_edges(keys, values, streams, slots):
+def pack_edges(keys, values, streams, slots, split):
     rows, columns = keys.shape
     tokens, channels = streams[0].shape
     edge = 2 * HALO
@@ -185,19 +185,36 @@
     first = pl.BlockSpec((edge, channels), lambda i: (0, 0))
     last = pl.BlockSpec((edge, channels), lambda i: (tokens // edge - 1, 0))
     halo = (count * HALO, channels)
-    laid = (slots, 2, rows, columns // slots)
+    laid = (2, rows, columns // slots)
     return pl.pallas_call(
-        pack_edges_kernel,
+        functools.partial(pack_edges_kernel, count, split),
         grid=(1,),
         in_specs=[whole] * 2 + [first] * count + [last] * count,
-        out_specs=[
-            pl.BlockSpec(laid, lambda i: (0, 0, 0, 0)),
-            pl.BlockSpec(halo, lambda i: (0, 0)),
-            pl.BlockSpec(halo, lambda i: (0, 0)),
-        ],
-        out_shape=[jax.ShapeDtypeStruct(shape, keys.dtype) for shape in (laid, halo, halo)],
+        out_specs=[pl.BlockSpec(laid, lambda i: (0, 0, 0))] * slots
+        + [pl.BlockSpec(halo, lambda i: (0, 0))] * 2,
+        out_shape=[jax.ShapeDtypeStruct(laid, keys.dtype)] * slots
+        + [jax.ShapeDtypeStruct(halo, keys.dtype)] * 2,
         name="pack_edges",
     )(keys, values, *streams, *streams)
+
+
+def join_kernel(split, *refs):
+    parts, target = refs[:-1], refs[-1]
+    piece = parts[0].shape[1]
+    slot = own_slot(split)
+    for distance, ref in enumerate(parts):
+        held = slot ^ distance
+        place = held % split * (len(parts) // split) + held // split
+        target[:, pl.ds(pl.multiple_of(place * piece, 32), piece)] = ref[...]
+
+
+def join(parts, split):
+    pair, rows, width = parts[0].shape
+    return pl.pallas_call(
+        functools.partial(join_kernel, split),
+        out_shape=jax.ShapeDtypeStruct((pair, rows * len(parts), width), parts[0].dtype),
+        name="join",
+    )(*parts)
 
 
 def pack_rows_kernel(split, q_ref, g_ref, *refs):
@@ -558,23 +575,13 @@
     ]
 
     streams = (gate_input, key_input, value_input, hyena_grad)
-    laid_kv, inner, outer = pack_edges(key_heads, value_heads, streams, slots)
+    *kv, inner, outer = pack_edges(key_heads, value_heads, streams, slots, split)
     inner = permute(inner, perm=[(i, i ^ 1) for i in range(ctx)])
     outer = permute(
         outer, perm=[(i, (i + 1 if i % 2 else i - 1)) for i in range(1, ctx - 1)]
     )
 
-    kv = share(laid_kv)
-    if piece % 32:
-        cut = [part.reshape(piece, slots, -1) for part in (query_heads, out_grad)]
-        laid = jnp.concatenate(cut, axis=2).transpose(1, 0, 2)
-        qg = share(laid).reshape(tp, split, piece, -1).transpose(1, 0, 2, 3)
-        qg = list(qg.reshape(split, tokens, -1))
-    else:
-        laid_kv, query_heads = lax.optimization_barrier((laid_kv, query_heads))
-        qg = list(pack_rows(query_heads, out_grad, slots, split))
-
-    def exchange(which):
+    def exchange(values, which):
         for distance in which:
             far_t, far_c = distance // split, distance % split
             perm = [
@@ -582,32 +589,42 @@
                 for t in range(tp)
                 for i in range(ctx)
             ]
-            qg[distance] = lax.ppermute(qg[distance], ("ctx", "tp"), perm)
+            values[distance] = lax.ppermute(values[distance], ("ctx", "tp"), perm)
+
+    pairwise = split > 1 and piece % 32 == 0
+    if pairwise:
+        kv[0], query_heads = lax.optimization_barrier((kv[0], query_heads))
+        qg = list(pack_rows(query_heads, out_grad, slots, split))
+        exchange(kv, range(1, slots))
+        kv[0], qg[0] = lax.optimization_barrier((kv[0], qg[0]))
+        own_kv = join(kv, split)
+    else:
+        kv = share(jnp.stack(kv)).reshape(tp, split, 2, piece, kv_local * HD)
+        own_kv = kv.transpose(2, 1, 0, 3, 4).reshape(2, unit, kv_local * HD)
+        cut = [part.reshape(piece, slots, -1) for part in (query_heads, out_grad)]
+        laid = jnp.concatenate(cut, axis=2).transpose(1, 0, 2)
+        qg = share(laid).reshape(tp, split, piece, -1).transpose(1, 0, 2, 3)
+        qg = list(qg.reshape(split, tokens, -1))
 
     calls = [(split - 1, 0), (split // 2, split // 2 - 1)] if split > 1 else [(0,)]
 
     def rows_for(call):
         return [a * split + c for c in calls[call] for a in range(tp)]
 
-    if piece % 32 == 0:
-        first = [d for d in rows_for(0) if d]
-    kv, inner, outer, qg[0] = lax.optimization_barrier((kv, inner, outer, qg[0]))
-    own_kv = kv.reshape(tp, split, 2, piece, kv_local * HD)
-    own_kv = own_kv.transpose(2, 1, 0, 3, 4).reshape(2, unit, kv_local * HD)
-
     filters = (short_filter, long_filter)
     columns = [own_kv]
-    if piece % 32 == 0:
+    if pairwise:
+        first = [d for d in rows_for(0) if d]
         own_kv, *held = lax.optimization_barrier((own_kv,) + tuple(qg[d] for d in first))
         columns = [own_kv]
         for distance, value in zip(first, held):
             qg[distance] = value
-        exchange(first)
+        exchange(qg, first)
     for hop in range(reach):
         coming = up(columns[-1])
         if hop == reach - 1:
             inner, columns[-1] = lax.optimization_barrier((inner, columns[-1]))
-            hyena_outs = hyena(streams, inner, outer, *filters, 0, 4)
+            hyena_outs = hyena(streams, inner, outer, *filters, 0, 1)
             coming, first_out = lax.optimization_barrier((coming, hyena_outs[0]))
             hyena_outs = [first_out] + list(hyena_outs[1:])
         columns.append(coming)
@@ -629,8 +646,8 @@
     arrived = None
     for call, distances in enumerate(calls):
         if call:
-            exchange(rows_for(call))
-        held = [qg[d] for d in rows_for(call)] if piece % 32 == 0 else qg
+            exchange(qg, rows_for(call))
+        held = [qg[d] for d in rows_for(call)] if pairwise else qg
         outs, terms = attention(held, pieces, info, record_lengths, distances, most, terms)
         if arrived is not None:
             at = 1 + reach * lanes
@@ -654,9 +671,10 @@
     running = plane_sum(reach).astype(bf16)
     for back in range(reach - 1, -1, -1):
         coming = down(running)
-        if back == reach - 1:
+        if back >= reach - 2:
             inner, running = lax.optimization_barrier((inner, running))
-            hyena_outs = hyena(streams, inner, outer, *filters, 4, 4, hyena_outs)
+            eighths = (1, 4) if back == reach - 1 else (5, 3)
+            hyena_outs = hyena(streams, inner, outer, *filters, *eighths, hyena_outs)
             coming, first_out = lax.optimization_barrier((coming, hyena_outs[0]))
             hyena_outs = [first_out] + list(hyena_outs[1:])
         running = plane_sum(back) + coming.astype(f32)

time: 145 us -> 148 us (1.021); the launches traced: 145 us -> 146 us
  waiting for transfers between devices: 44.4 us -> 38.9 us
  starting transfers between devices: 34.8 us -> 38.7 us
  local copies, waits for them, and re-layouts: 7.67 us -> 9.91 us
    ppermute x2, waiting for transfers between devices: 27.9 us -> 12.7 us  [down(): return permute(values, perm=[(i + PLANE, i) for i in range(ctx - PLANE)])]
    ppermute x7 -> x14, starting transfers between devices: 6.66 us -> 18.4 us  [exchange(): values[distance] = lax.ppermute(values[distance], ('ctx', 'tp'), perm)]
    ppermute x1, waiting for transfers between devices: 1.07 us -> 10.7 us  [body(): tail_term = permute(terms[0], perm=[(j, i) for i, j in far_pairs])]
    all_to_all x1 -> x0, starting transfers between devices: 5.17 us -> none  [share(): lax.all_to_all(laid, ('tp', 'ctx'), 0, 0, axis_index_groups=members, tile...]
    pallas_call x2, Pallas kernels: 30.5 us -> 25.8 us  [attention(): pl.pallas_call(functools.partial(attention_kernel, pieces, distances, gro...]
    ppermute x2, starting transfers between devices: 7.91 us -> 4.81 us  [up(): return permute(values, perm=[(i, i + PLANE) for i in range(ctx - PLANE)])]
    all_to_all x1 -> x0, waiting for transfers between devices: 2.73 us -> none  [share(): lax.all_to_all(laid, ('tp', 'ctx'), 0, 0, axis_index_groups=members, tile...]
    ppermute x6, waiting for transfers between devices: 3.84 us -> 6.52 us  [swap(): return permute(values, perm=[(i, i ^ distance) for i in range(ctx)])]
  transfers between devices with their start and end apart: 22 -> 28, of which waited for: 9 -> 10; matrix products, arithmetic and copies ran while one was open for 1% -> 2% of each run, Pallas kernels for 37% -> 35%
where the time goes in v1:
time: 148 us; the launch traced here: 146 us
  Pallas kernels  54.6 us (37%)
  waiting for transfers between devices  38.9 us (26%)
  starting transfers between devices  38.7 us (26%)
  local copies, waits for them, and re-layouts  9.91 us (7%)
  other arithmetic  2.79 us (2%)
    pallas_call x2, Pallas kernels, attention(): pl.pallas_call(functools.partial(attention_kernel, pieces, distances, gro...  25.8 us
    ppermute x14, starting transfers between devices, exchange(): values[distance] = lax.ppermute(values[distance], ('ctx', 'tp'), perm)  18.4 us
    pallas_call x3, Pallas kernels, hyena(): pl.pallas_call(functools.partial(hyena_kernel, first * width), grid=(step...  17.4 us
    ppermute x2, waiting for transfers between devices, down(): return permute(values, perm=[(i + PLANE, i) for i in range(ctx - PLANE)])  12.7 us
    ppermute x1, waiting for transfers between devices, body(): tail_term = permute(terms[0], perm=[(j, i) for i, j in far_pairs])  10.7 us
    unnamed x66, local copies, waits for them, and re-layouts  8.1 us
    ppermute x6, waiting for transfers between devices, swap(): return permute(values, perm=[(i, i ^ distance) for i in range(ctx)])  6.52 us
    ppermute x1, starting transfers between devices, body(): tail_kv = permute(tail_kv, perm=far_pairs)  6.3 us
  transfers between devices with their start and end apart: 28, of which 10 were waited for; matrix products, arithmetic and copies ran while one was open for 2% of the time, Pallas kernels for 35%

profile of v1, /device:TPU:0, one launch (start us, length us, event | category | flops | bytes accessed | tf_op | source)
XLA Modules:
  0.0 146.0 jit_solution(7640569515657110531)
XLA Ops:
  0.6 2.4 %pack_edges.1 = (bf16[2,96,128]{2,1,0:T(8,128)(2,1)}, bf16[2,96,128]{2,1,0:T(8,128)(2,1)}, bf16[2,96,128]{2,1,0:T(8,128)(2,1)}, bf16[2,96,128]{2,1,0:T(8,128)(2,...) custom-call(bf16[96,1024]{1,0:T(8,128)(2,1)} %k_ref.1, ...), custom_call_target="tpu_custom_call" | custom-call | tf_op jit(solution)/shard_map/pack_edges/pallas_call | solution.py:189
  3.1 3.3 %collective-permute-start.10 = (bf16[2,96,128]{2,1,0:T(8,128)(2,1)}, bf16[2,96,128]{2,1,0:T(8,128)(2,1)S(1)}, u32[]{:S(2)}, u32[]{:S(2)}) collective-permute-start(bf16[2,96,128]{2,1,0:T(8,128)(2,1)} %get-tuple-element.91), channel_id=1, source_target_pairs={{0,7},{2,5},{4,3},{6,1},{8,15},{10,13},{12,11},{14,9},{16,23},{18,... | collective-permute-start | bytes 147464 | tf_op jit(solution)/shard_map/ppermute | solution.py:592
  8.9 1.9 %collective-permute-start.8 = (bf16[2,96,128]{2,1,0:T(8,128)(2,1)}, bf16[2,96,128]{2,1,0:T(8,128)(2,1)S(1)}, u32[]{:S(2)}, u32[]{:S(2)}) collective-permute-start(bf16[2,96,128]{2,1,0:T(8,128)(2,1)} %get-tuple-element.89), channel_id=1, source_target_pairs={{0,3},{2,1},{4,7},{6,5},{8,11},{10,9},{12,15},{14,13},{16,19},{18,... | collective-permute-start | bytes 147464 | tf_op jit(solution)/shard_map/ppermute | solution.py:592
  10.9 1.4 collective-permute-start.9
  12.3 3.8 %pack_rows.1 = (bf16[96,2048]{1,0:T(8,128)(2,1)}, bf16[96,2048]{1,0:T(8,128)(2,1)}, bf16[96,2048]{1,0:T(8,128)(2,1)}, bf16[96,2048]{1,0:T(8,128)(2,1)}, bf16[96,...) custom-call(bf16[96,8192]{1,0:T(8,128)(2,1)} %q_ref, ...), custom_call_target="tpu_custom_call" | custom-call | tf_op jit(solution)/shard_map/pack_rows/pallas_call | solution.py:242
  17.5 1.8 %join.1.refs_7_ = bf16[2,768,128]{2,1,0:T(8,128)(2,1)} custom-call(bf16[2,96,128]{2,1,0:T(8,128)(2,1)} %get-tuple-element.84.refs_0_, bf16[2,96,128]{2,1,0:T(8,128)(2,1)} %copy-done.23, bf16[2,96,128]{2,1,0:T(8,128)(2,1)} %copy-done.24, bf16[2,96,128]{2,1,0:T(8,128)(2,1)} %copy-done.25, bf16[2,96,128]{2,1,0:T(8,128)(2,1)} %copy-done.26, ...), custom_call_target="tpu_custom_call" | custom-call | tf_op jit(solution)/shard_map/join/pallas_call | solution.py:213
  19.3 3.5 %collective-permute-start.12 = (bf16[2,768,128]{2,1,0:T(8,128)(2,1)}, bf16[2,768,128]{2,1,0:T(8,128)(2,1)S(1)}, u32[]{:S(2)}, u32[]{:S(2)}) collective-permute-start(bf16[2,768,128]{2,1,0:T(8,128)(2,1)} %join.1.refs_7_), channel_id=1, source_target_pairs={{0,8},{2,10},{4,12},{6,14},{8,16},{10,18},{12,20},{14,22},{16,24},... | collective-permute-start | bytes 1179656 | tf_op jit(solution)/shard_map/ppermute | solution.py:564
  24.5 4.0 %collective-permute-start.16 = (bf16[96,2048]{1,0:T(8,128)(2,1)}, bf16[96,2048]{1,0:T(8,128)(2,1)S(1)}, u32[]{:S(2)}, u32[]{:S(2)}) collective-permute-start(bf16[96,2048]{1,0:T(8,128)(2,1)} %get-tuple-element.104), channel_id=1, source_target_pairs={{0,6},{2,4},{4,2},{6,0},{8,14},{10,12},{12,10},{14,8},{16,22},{18,... | collective-permute-start | bytes 1179656 | tf_op jit(solution)/shard_map/ppermute | solution.py:592
  30.0 1.7 %collective-permute-done.12.refs_8_ = bf16[2,768,128]{2,1,0:T(8,128)(2,1)S(1)} collective-permute-done((bf16[2,768,128]{2,1,0:T(8,128)(2,1)}, bf16[2,768,128]{2,1,0:T(8,128)(2,1)S(1)}, u32[]{:S(2)}, u32[]{:S(2)}) %collective-permute-start.12) | collective-permute-done | bytes 393248 | tf_op jit(solution)/shard_map/ppermute | solution.py:564
  31.7 6.3 %collective-permute-start.13 = (bf16[2,192,128]{2,1,0:T(8,128)(2,1)S(1)}, bf16[2,192,128]{2,1,0:T(8,128)(2,1)S(1)}, u32[]{:S(2)}, u32[]{:S(2)}) collective-permute-start(bf16[2,192,128]{2,1,0:T(8,128)(2,1)S(1)} %slice.16), channel_id=1, source_target_pairs={{0,24},{2,26},{4,28},{6,30},{1,25},{3,27},{5,29},{7,31}} | collective-permute-start | bytes 294920 | tf_op jit(solution)/shard_map/ppermute | solution.py:633
  38.0 1.3 collective-permute-start.14
  39.4 1.4 copy-done.1
  40.8 1.4 copy-done.4
  43.2 3.3 %hyena.3 = (bf16[192,4096]{1,0:T(8,128)(2,1)}, bf16[192,4096]{1,0:T(8,128)(2,1)}, bf16[192,4096]{1,0:T(8,128)(2,1)}, bf16[192,4096]{1,0:T(8,128)(2,1)}) custom-call(bf16[192,4096]{1,0:T(8,128)(2,1)S(1)} %copy-done, bf16[192,4096]{1,0:T(8,128)(2,1)S(1)} %copy-done.1, bf16[192,4096]{1,0:T(8,128)(2,1)S(1)} %copy-done.4, bf16[192,4096]{1,0:T(8,128)(2,1)} %grad_ref.5, ...), custom_call_target="tpu_custom_call" | custom-call | flops 5505024000 | bytes 1572864 | tf_op jit(solution)/shard_map/hyena/pallas_call | solution.py:127
  46.5 2.1 %collective-permute-done.14.refs_9_ = bf16[2,768,128]{2,1,0:T(8,128)(2,1)S(1)} collective-permute-done((bf16[2,768,128]{2,1,0:T(8,128)(2,1)S(1)}, bf16[2,768,128]{2,1,0:T(8,128)(2,1)S(1)}, u32[]{:S(2)}, u32[]{:S(2)}) %collective-permute-start.14) | collective-permute-done | bytes 393248 | tf_op jit(solution)/shard_map/ppermute | solution.py:564
  48.6 3.0 %collective-permute-start.1 = (bf16[96,2048]{1,0:T(8,128)(2,1)S(1)}, bf16[96,2048]{1,0:T(8,128)(2,1)S(1)}, u32[]{:S(2)}, u32[]{:S(2)}) collective-permute-start(bf16[96,2048]{1,0:T(8,128)(2,1)S(1)} %copy-done.31), channel_id=1, source_target_pairs={{0,5},{2,7},{4,1},{6,3},{8,13},{10,15},{12,9},{14,11},{16,21},{18,... | collective-permute-start | bytes 1179656 | tf_op jit(solution)/shard_map/ppermute | solution.py:592
  52.2 13.1 %attention.2 = (bf16[192,2048]{1,0:T(8,128)(2,1)S(1)}, bf16[192,2048]{1,0:T(8,128)(2,1)S(1)}, bf16[2,192,128]{2,1,0:T(8,128)(2,1)S(1)}, bf16[2,768,128]{2,1,0:T(...) custom-call(s32[5]{0:T(128)S(1)} %stack.10.refs_0_, s32[16]{0:T(128)S(1)} %copy-done.21, ...), custom_call_target="tpu_custom_call" | custom-call | flops 48318382080 | bytes 12582912 | tf_op jit(solution)/shard_map/attention/pallas_call | solution.py:452
  65.7 2.6 %collective-permute-done.1.refs_3_ = bf16[96,2048]{1,0:T(8,128)(2,1)S(1)} collective-permute-done((bf16[96,2048]{1,0:T(8,128)(2,1)S(1)}, bf16[96,2048]{1,0:T(8,128)(2,1)S(1)}, u32[]{:S(2)}, u32[]{:S(2)}) %collective-permute-start.1) | collective-permute-done | bytes 393248 | tf_op jit(solution)/shard_map/ppermute | solution.py:592
  68.3 2.6 %collective-permute-done.3.refs_5_ = bf16[96,2048]{1,0:T(8,128)(2,1)S(1)} collective-permute-done((bf16[96,2048]{1,0:T(8,128)(2,1)S(1)}, bf16[96,2048]{1,0:T(8,128)(2,1)S(1)}, u32[]{:S(2)}, u32[]{:S(2)}) %collective-permute-start.3) | collective-permute-done | bytes 393248 | tf_op jit(solution)/shard_map/ppermute | solution.py:592
  71.9 12.7 %attention.3 = (bf16[192,2048]{1,0:T(8,128)(2,1)}, bf16[192,2048]{1,0:T(8,128)(2,1)}, bf16[2,192,128]{2,1,0:T(8,128)(2,1)S(1)}, bf16[2,768,128]{2,1,0:T(8,128)(2...) custom-call(s32[5]{0:T(128)S(1)} %stack.10.refs_0_, s32[16]{0:T(128)S(1)} %copy-done.21, ...), custom_call_target="tpu_custom_call" | custom-call | flops 48318382080 | bytes 12582912 | tf_op jit(solution)/shard_map/attention/pallas_call | solution.py:452
  84.6 2.4 %collective-permute-start.22 = (bf16[192,2048]{1,0:T(8,128)(2,1)}, bf16[192,2048]{1,0:T(8,128)(2,1)}, u32[]{:S(2)}, u32[]{:S(2)}) collective-permute-start(bf16[192,2048]{1,0:T(8,128)(2,1)} %get-tuple-element.132), channel_id=1, source_target_pairs={{0,2},{2,0},{4,6},{6,4},{8,10},{10,8},{12,14},{14,12},{16,18},{18,... | collective-permute-start | bytes 2359304 | tf_op jit(solution)/shard_map/ppermute | solution.py:570
  87.1 1.3 collective-permute-start.20
  88.4 7.6 %hyena.4 = (bf16[192,4096]{1,0:T(8,128)(2,1)}, bf16[192,4096]{1,0:T(8,128)(2,1)}, bf16[192,4096]{1,0:T(8,128)(2,1)}, bf16[192,4096]{1,0:T(8,128)(2,1)}) custom-call(bf16[192,4096]{1,0:T(8,128)(2,1)S(1)} %copy-done, bf16[192,4096]{1,0:T(8,128)(2,1)S(1)} %copy-done.2, ...), custom_call_target="tpu_custom_call", output_to_operand_aliasing={{0}: (8, {}), {1}: (9, {}), {2}: (10, {}), {3}: (11, {})} | custom-call | flops 5505024000 | bytes 6291456 | tf_op jit(solution)/shard_map/hyena/pallas_call | solution.py:127
  96.1 4.6 %collective-permute-done.20 = bf16[2,768,128]{2,1,0:T(8,128)(2,1)S(1)} collective-permute-done((bf16[2,768,128]{2,1,0:T(8,128)(2,1)S(1)}, bf16[2,768,128]{2,1,0:T(8,128)(2,1)S(1)}, u32[]{:S(2)}, u32[]{:S(2)}) %collective-permute-start.20) | collective-permute-done | bytes 393248 | tf_op jit(solution)/shard_map/ppermute | solution.py:567
  102.8 1.3 collective-permute-start.24
  104.2 2.7 %collective-permute-done.23.refs_2_ = bf16[192,2048]{1,0:T(8,128)(2,1)} collective-permute-done((bf16[192,2048]{1,0:T(8,128)(2,1)}, bf16[192,2048]{1,0:T(8,128)(2,1)}, u32[]{:S(2)}, u32[]{:S(2)}) %collective-permute-start.23) | collective-permute-done | bytes 786464 | tf_op jit(solution)/shard_map/ppermute | solution.py:570
  108.0 3.4 %settle.1 = (bf16[192,4096]{1,0:T(8,128)(2,1)}, bf16[192,4096]{1,0:T(8,128)(2,1)}) custom-call(bf16[192,2048]{1,0:T(8,128)(2,1)S(1)} %get-tuple-element.131.refs_0_, bf16[192,2048]{1,0:T(8,128)(2,1)} %collective-permute-done.22.refs_1_, bf16[192,2048]{1,0:T(8,128)(2,1)} %collective-permute-done.23.refs_2_, bf16[192,2048]{1,0:T(8,128)(2,1)S(1)} %copy-done.8), custom_call_target="tpu_custom_call" | custom-call | tf_op jit(solution)/shard_map/settle/pallas_call | solution.py:505
  112.3 6.4 %hyena.5 = (bf16[192,4096]{1,0:T(8,128)(2,1)}, bf16[192,4096]{1,0:T(8,128)(2,1)}, bf16[192,4096]{1,0:T(8,128)(2,1)}, bf16[192,4096]{1,0:T(8,128)(2,1)}) custom-call(bf16[192,4096]{1,0:T(8,128)(2,1)S(1)} %copy-done, bf16[192,4096]{1,0:T(8,128)(2,1)S(1)} %copy-done.3, ...), custom_call_target="tpu_custom_call", output_to_operand_aliasing={{0}: (8, {}), {1}: (9, {}), {2}: (10, {}), {3}: (11, {})} | custom-call | flops 4128768000 | bytes 4718592 | tf_op jit(solution)/shard_map/hyena/pallas_call | solution.py:127
  118.7 8.0 %collective-permute-done.21 = bf16[2,768,128]{2,1,0:T(8,128)(2,1)} collective-permute-done((bf16[2,768,128]{2,1,0:T(8,128)(2,1)}, bf16[2,768,128]{2,1,0:T(8,128)(2,1)}, u32[]{:S(2)}, u32[]{:S(2)}) %collective-permute-start.21) | collective-permute-done | bytes 393248 | tf_op jit(solution)/shard_map/ppermute | solution.py:567
  127.9 10.7 %collective-permute-done.24 = bf16[2,192,128]{2,1,0:T(8,128)(2,1)S(1)} collective-permute-done((bf16[2,192,128]{2,1,0:T(8,128)(2,1)}, bf16[2,192,128]{2,1,0:T(8,128)(2,1)S(1)}, u32[]{:S(2)}, u32[]{:S(2)}) %collective-permute-start.24) | collective-permute-done | bytes 98336 | tf_op jit(solution)/shard_map/ppermute | solution.py:670
  139.6 1.5 collective-permute-start.27
  141.1 2.6 %collective-permute-done.25 = bf16[2,192,128]{2,1,0:T(8,128)(2,1)S(1)} collective-permute-done((bf16[2,192,128]{2,1,0:T(8,128)(2,1)S(1)}, bf16[2,192,128]{2,1,0:T(8,128)(2,1)S(1)}, u32[]{:S(2)}, u32[]{:S(2)}) %collective-permute-start.25) | collective-permute-done | bytes 98336 | tf_op jit(solution)/shard_map/ppermute | solution.py:570
  (110 shorter events, 18.6 us)
Async XLA Ops:
  3.1 5.9 %collective-permute-start.10 = (bf16[2,96,128]{2,1,0:T(8,128)(2,1)}, bf16[2,96,128]{2,1,0:T(8,128)(2,1)S(1)}, u32[]{:S(2)}, u32[]{:S(2)}) collective-permute-start(bf16[2,96,128]{2,1,0:T(8,128)(2,1)} %get-tuple-element.91), channel_id=1, source_target_pairs={{0,7},{2,5},{4,3},{6,1},{8,15},{10,13},{12,11},{14,9},{16,23},{18,... | collective-permute-start | bytes 147464 | tf_op jit(solution)/shard_map/ppermute | solution.py:592
  6.4 4.5 %collective-permute-start.4 = (bf16[2,96,128]{2,1,0:T(8,128)(2,1)}, bf16[2,96,128]{2,1,0:T(8,128)(2,1)S(1)}, u32[]{:S(2)}, u32[]{:S(2)}) collective-permute-start(bf16[2,96,128]{2,1,0:T(8,128)(2,1)} %get-tuple-element.85), channel_id=1, source_target_pairs={{0,2},{2,0},{4,6},{6,4},{8,10},{10,8},{12,14},{14,12},{16,18},{18,... | collective-permute-start | bytes 147464 | tf_op jit(solution)/shard_map/ppermute | solution.py:592
  7.1 9.1 %collective-permute-start.5 = (bf16[2,96,128]{2,1,0:T(8,128)(2,1)}, bf16[2,96,128]{2,1,0:T(8,128)(2,1)S(1)}, u32[]{:S(2)}, u32[]{:S(2)}) collective-permute-start(bf16[2,96,128]{2,1,0:T(8,128)(2,1)} %get-tuple-element.86), channel_id=1, source_target_pairs={{0,4},{2,6},{4,0},{6,2},{8,12},{10,14},{12,8},{14,10},{16,20},{18,... | collective-permute-start | bytes 147464 | tf_op jit(solution)/shard_map/ppermute | solution.py:592
  7.6 8.6 %collective-permute-start.6 = (bf16[2,96,128]{2,1,0:T(8,128)(2,1)}, bf16[2,96,128]{2,1,0:T(8,128)(2,1)S(1)}, u32[]{:S(2)}, u32[]{:S(2)}) collective-permute-start(bf16[2,96,128]{2,1,0:T(8,128)(2,1)} %get-tuple-element.87), channel_id=1, source_target_pairs={{0,6},{2,4},{4,2},{6,0},{8,14},{10,12},{12,10},{14,8},{16,22},{18,... | collective-permute-start | bytes 147464 | tf_op jit(solution)/shard_map/ppermute | solution.py:592
  8.4 7.8 %collective-permute-start.7 = (bf16[2,96,128]{2,1,0:T(8,128)(2,1)}, bf16[2,96,128]{2,1,0:T(8,128)(2,1)S(1)}, u32[]{:S(2)}, u32[]{:S(2)}) collective-permute-start(bf16[2,96,128]{2,1,0:T(8,128)(2,1)} %get-tuple-element.88), channel_id=1, source_target_pairs={{0,1},{2,3},{4,5},{6,7},{8,9},{10,11},{12,13},{14,15},{16,17},{18,... | collective-permute-start | bytes 147464 | tf_op jit(solution)/shard_map/ppermute | solution.py:592
  8.9 7.3 %collective-permute-start.8 = (bf16[2,96,128]{2,1,0:T(8,128)(2,1)}, bf16[2,96,128]{2,1,0:T(8,128)(2,1)S(1)}, u32[]{:S(2)}, u32[]{:S(2)}) collective-permute-start(bf16[2,96,128]{2,1,0:T(8,128)(2,1)} %get-tuple-element.89), channel_id=1, source_target_pairs={{0,3},{2,1},{4,7},{6,5},{8,11},{10,9},{12,15},{14,13},{16,19},{18,... | collective-permute-start | bytes 147464 | tf_op jit(solution)/shard_map/ppermute | solution.py:592
  10.9 5.3 %collective-permute-start.9 = (bf16[2,96,128]{2,1,0:T(8,128)(2,1)}, bf16[2,96,128]{2,1,0:T(8,128)(2,1)S(1)}, u32[]{:S(2)}, u32[]{:S(2)}) collective-permute-start(bf16[2,96,128]{2,1,0:T(8,128)(2,1)} %get-tuple-element.90), channel_id=1, source_target_pairs={{0,5},{2,7},{4,1},{6,3},{8,13},{10,15},{12,9},{14,11},{16,21},{18,... | collective-permute-start | bytes 147464 | tf_op jit(solution)/shard_map/ppermute | solution.py:592
  12.3 27.0 %copy-start = (bf16[192,4096]{1,0:T(8,128)(2,1)S(1)}, bf16[192,4096]{1,0:T(8,128)(2,1)}, u32[]{:S(2)}) copy-start(bf16[192,4096]{1,0:T(8,128)(2,1)} %gate_ref.5) | copy-start | bytes 4718596
  12.3 27.0 %copy-start.20 = (f32[7,256]{1,0:T(8,128)S(1)}, f32[7,256]{1,0:T(8,128)}, u32[]{:S(2)}) copy-start(f32[7,256]{1,0:T(8,128)} %long_ref.5) | copy-start | bytes 21508
  19.3 12.5 %collective-permute-start.12 = (bf16[2,768,128]{2,1,0:T(8,128)(2,1)}, bf16[2,768,128]{2,1,0:T(8,128)(2,1)S(1)}, u32[]{:S(2)}, u32[]{:S(2)}) collective-permute-start(bf16[2,768,128]{2,1,0:T(8,128)(2,1)} %join.1.refs_7_), channel_id=1, source_target_pairs={{0,8},{2,10},{4,12},{6,14},{8,16},{10,18},{12,20},{14,22},{16,24},... | collective-permute-start | bytes 1179656 | tf_op jit(solution)/shard_map/ppermute | solution.py:564
  22.8 6.8 %collective-permute-start.11 = (bf16[32,4096]{1,0:T(8,128)(2,1)}, bf16[32,4096]{1,0:T(8,128)(2,1)S(1)}, u32[]{:S(2)}, u32[]{:S(2)}) collective-permute-start(bf16[32,4096]{1,0:T(8,128)(2,1)} %get-tuple-element.96), channel_id=1, source_target_pairs={{0,2},{2,0},{4,6},{6,4},{8,10},{10,8},{12,14},{14,12},{16,18},{18,... | collective-permute-start | bytes 786440 | tf_op jit(solution)/shard_map/ppermute | solution.py:579
  22.8 15.2 %collective-permute-start.15 = (bf16[32,4096]{1,0:T(8,128)(2,1)}, bf16[32,4096]{1,0:T(8,128)(2,1)S(1)}, u32[]{:S(2)}, u32[]{:S(2)}) collective-permute-start(bf16[32,4096]{1,0:T(8,128)(2,1)} %get-tuple-element.101), channel_id=1, source_target_pairs={{2,4},{4,2},{6,8},{8,6},{10,12},{12,10},{14,16},{16,14},{18,20},{2... | collective-permute-start | bytes 786440 | tf_op jit(solution)/shard_map/ppermute | solution.py:580
  23.6 28.6 %copy-start.21 = (s32[16]{0:T(128)S(1)}, s32[16]{0:T(128)}, u32[]{:S(2)}) copy-start(s32[16]{0:T(128)} %refs_1_.5) | copy-start | bytes 196
  24.5 24.0 %collective-permute-start.16 = (bf16[96,2048]{1,0:T(8,128)(2,1)}, bf16[96,2048]{1,0:T(8,128)(2,1)S(1)}, u32[]{:S(2)}, u32[]{:S(2)}) collective-permute-start(bf16[96,2048]{1,0:T(8,128)(2,1)} %get-tuple-element.104), channel_id=1, source_target_pairs={{0,6},{2,4},{4,2},{6,0},{8,14},{10,12},{12,10},{14,8},{16,22},{18,... | collective-permute-start | bytes 1179656 | tf_op jit(solution)/shard_map/ppermute | solution.py:592
  28.5 23.0 %collective-permute-start.17 = (bf16[96,2048]{1,0:T(8,128)(2,1)}, bf16[96,2048]{1,0:T(8,128)(2,1)S(1)}, u32[]{:S(2)}, u32[]{:S(2)}) collective-permute-start(bf16[96,2048]{1,0:T(8,128)(2,1)} %get-tuple-element.105), channel_id=1, source_target_pairs={{0,7},{2,5},{4,3},{6,1},{8,15},{10,13},{12,11},{14,9},{16,23},{18,... | collective-permute-start | bytes 1179656 | tf_op jit(solution)/shard_map/ppermute | solution.py:592
  29.5 22.0 %collective-permute-start.18 = (bf16[96,2048]{1,0:T(8,128)(2,1)}, bf16[96,2048]{1,0:T(8,128)(2,1)S(1)}, u32[]{:S(2)}, u32[]{:S(2)}) collective-permute-start(bf16[96,2048]{1,0:T(8,128)(2,1)} %get-tuple-element.107), channel_id=1, source_target_pairs={{0,1},{2,3},{4,5},{6,7},{8,9},{10,11},{12,13},{14,15},{16,17},{18,... | collective-permute-start | bytes 1179656 | tf_op jit(solution)/shard_map/ppermute | solution.py:592
  31.7 20.5 %collective-permute-start.13 = (bf16[2,192,128]{2,1,0:T(8,128)(2,1)S(1)}, bf16[2,192,128]{2,1,0:T(8,128)(2,1)S(1)}, u32[]{:S(2)}, u32[]{:S(2)}) collective-permute-start(bf16[2,192,128]{2,1,0:T(8,128)(2,1)S(1)} %slice.16), channel_id=1, source_target_pairs={{0,24},{2,26},{4,28},{6,30},{1,25},{3,27},{5,29},{7,31}} | collective-permute-start | bytes 294920 | tf_op jit(solution)/shard_map/ppermute | solution.py:633
  38.0 10.5 %collective-permute-start.14 = (bf16[2,768,128]{2,1,0:T(8,128)(2,1)S(1)}, bf16[2,768,128]{2,1,0:T(8,128)(2,1)S(1)}, u32[]{:S(2)}, u32[]{:S(2)}) collective-permute-start(bf16[2,768,128]{2,1,0:T(8,128)(2,1)S(1)} %collective-permute-done.12.refs_8_), channel_id=1, source_target_pairs={{0,8},{2,10},{4,12},{6,14},{8,16},{10,18},{12,20},{14,22},{16,24},... | collective-permute-start | bytes 1179656 | tf_op jit(solution)/shard_map/ppermute | solution.py:564
  48.6 17.1 %collective-permute-start = (bf16[96,2048]{1,0:T(8,128)(2,1)S(1)}, bf16[96,2048]{1,0:T(8,128)(2,1)S(1)}, u32[]{:S(2)}, u32[]{:S(2)}) collective-permute-start(bf16[96,2048]{1,0:T(8,128)(2,1)S(1)} %copy-done.32), channel_id=1, source_target_pairs={{0,4},{2,6},{4,0},{6,2},{8,12},{10,14},{12,8},{14,10},{16,20},{18,... | collective-permute-start | bytes 1179656 | tf_op jit(solution)/shard_map/ppermute | solution.py:592
  48.6 19.7 %collective-permute-start.1 = (bf16[96,2048]{1,0:T(8,128)(2,1)S(1)}, bf16[96,2048]{1,0:T(8,128)(2,1)S(1)}, u32[]{:S(2)}, u32[]{:S(2)}) collective-permute-start(bf16[96,2048]{1,0:T(8,128)(2,1)S(1)} %copy-done.31), channel_id=1, source_target_pairs={{0,5},{2,7},{4,1},{6,3},{8,13},{10,15},{12,9},{14,11},{16,21},{18,... | collective-permute-start | bytes 1179656 | tf_op jit(solution)/shard_map/ppermute | solution.py:592
  51.6 16.7 %collective-permute-start.2 = (bf16[96,2048]{1,0:T(8,128)(2,1)S(1)}, bf16[96,2048]{1,0:T(8,128)(2,1)S(1)}, u32[]{:S(2)}, u32[]{:S(2)}) collective-permute-start(bf16[96,2048]{1,0:T(8,128)(2,1)S(1)} %copy-done.30), channel_id=1, source_target_pairs={{0,2},{2,0},{4,6},{6,4},{8,10},{10,8},{12,14},{14,12},{16,18},{18,... | collective-permute-start | bytes 1179656 | tf_op jit(solution)/shard_map/ppermute | solution.py:592
  51.6 19.3 %collective-permute-start.3 = (bf16[96,2048]{1,0:T(8,128)(2,1)S(1)}, bf16[96,2048]{1,0:T(8,128)(2,1)S(1)}, u32[]{:S(2)}, u32[]{:S(2)}) collective-permute-start(bf16[96,2048]{1,0:T(8,128)(2,1)S(1)} %copy-done.29), channel_id=1, source_target_pairs={{0,3},{2,1},{4,7},{6,5},{8,11},{10,9},{12,15},{14,13},{16,19},{18,... | collective-permute-start | bytes 1179656 | tf_op jit(solution)/shard_map/ppermute | solution.py:592
  65.4 21.7 %collective-permute-start.19 = (bf16[192,2048]{1,0:T(8,128)(2,1)S(1)}, bf16[192,2048]{1,0:T(8,128)(2,1)S(1)}, u32[]{:S(2)}, u32[]{:S(2)}) collective-permute-start(bf16[192,2048]{1,0:T(8,128)(2,1)S(1)} %get-tuple-element.114), channel_id=1, source_target_pairs={{0,6},{2,4},{4,2},{6,0},{8,14},{10,12},{12,10},{14,8},{16,22},{18,... | collective-permute-start | bytes 2359304 | tf_op jit(solution)/shard_map/ppermute | solution.py:570
  84.6 19.5 %collective-permute-start.22 = (bf16[192,2048]{1,0:T(8,128)(2,1)}, bf16[192,2048]{1,0:T(8,128)(2,1)}, u32[]{:S(2)}, u32[]{:S(2)}) collective-permute-start(bf16[192,2048]{1,0:T(8,128)(2,1)} %get-tuple-element.132), channel_id=1, source_target_pairs={{0,2},{2,0},{4,6},{6,4},{8,10},{10,8},{12,14},{14,12},{16,18},{18,... | collective-permute-start | bytes 2359304 | tf_op jit(solution)/shard_map/ppermute | solution.py:570
  87.1 19.8 %collective-permute-start.23 = (bf16[192,2048]{1,0:T(8,128)(2,1)}, bf16[192,2048]{1,0:T(8,128)(2,1)}, u32[]{:S(2)}, u32[]{:S(2)}) collective-permute-start(bf16[192,2048]{1,0:T(8,128)(2,1)} %get-tuple-element.133), channel_id=1, source_target_pairs={{0,4},{2,6},{4,0},{6,2},{8,12},{10,14},{12,8},{14,10},{16,20},{18,... | collective-permute-start | bytes 2359304 | tf_op jit(solution)/shard_map/ppermute | solution.py:570
  87.1 13.6 %collective-permute-start.20 = (bf16[2,768,128]{2,1,0:T(8,128)(2,1)S(1)}, bf16[2,768,128]{2,1,0:T(8,128)(2,1)S(1)}, u32[]{:S(2)}, u32[]{:S(2)}) collective-permute-start(bf16[2,768,128]{2,1,0:T(8,128)(2,1)S(1)} %get-tuple-element.116), channel_id=1, source_target_pairs={{8,0},{10,2},{12,4},{14,6},{16,8},{18,10},{20,12},{22,14},{24,16},... | collective-permute-start | bytes 1179656 | tf_op jit(solution)/shard_map/ppermute | solution.py:567
  88.4 23.0 %copy-start.15 = (bf16[32,4096]{1,0:T(8,128)(2,1)S(1)}, bf16[32,4096]{1,0:T(8,128)(2,1)}, u32[]{:S(2)}) copy-start(bf16[32,4096]{1,0:T(8,128)(2,1)} %copy-done.13) | copy-start | bytes 786436
  101.5 25.2 %collective-permute-start.21 = (bf16[2,768,128]{2,1,0:T(8,128)(2,1)}, bf16[2,768,128]{2,1,0:T(8,128)(2,1)}, u32[]{:S(2)}, u32[]{:S(2)}) collective-permute-start(bf16[2,768,128]{2,1,0:T(8,128)(2,1)} %add_convert_fusion), channel_id=1, source_target_pairs={{8,0},{10,2},{12,4},{14,6},{16,8},{18,10},{20,12},{22,14},{24,16},... | collective-permute-start | bytes 1179656 | tf_op jit(solution)/shard_map/ppermute | solution.py:567
  102.8 35.7 %collective-permute-start.24 = (bf16[2,192,128]{2,1,0:T(8,128)(2,1)}, bf16[2,192,128]{2,1,0:T(8,128)(2,1)S(1)}, u32[]{:S(2)}, u32[]{:S(2)}) collective-permute-start(bf16[2,192,128]{2,1,0:T(8,128)(2,1)} %copy-done.19), channel_id=1, source_target_pairs={{24,0},{26,2},{28,4},{30,6},{25,1},{27,3},{29,5},{31,7}} | collective-permute-start | bytes 294920 | tf_op jit(solution)/shard_map/ppermute | solution.py:670
  139.2 4.5 %collective-permute-start.25 = (bf16[2,192,128]{2,1,0:T(8,128)(2,1)S(1)}, bf16[2,192,128]{2,1,0:T(8,128)(2,1)S(1)}, u32[]{:S(2)}, u32[]{:S(2)}) collective-permute-start(bf16[2,192,128]{2,1,0:T(8,128)(2,1)S(1)} %get-tuple-element.152), channel_id=1, source_target_pairs={{0,6},{2,4},{4,2},{6,0},{8,14},{10,12},{12,10},{14,8},{16,22},{18,... | collective-permute-start | bytes 294920 | tf_op jit(solution)/shard_map/ppermute | solution.py:570
  139.2 5.7 %collective-permute-start.26 = (bf16[2,192,128]{2,1,0:T(8,128)(2,1)S(1)}, bf16[2,192,128]{2,1,0:T(8,128)(2,1)S(1)}, u32[]{:S(2)}, u32[]{:S(2)}) collective-permute-start(bf16[2,192,128]{2,1,0:T(8,128)(2,1)S(1)} %get-tuple-element.153), channel_id=1, source_target_pairs={{0,4},{2,6},{4,0},{6,2},{8,12},{10,14},{12,8},{14,10},{16,20},{18,... | collective-permute-start | bytes 294920 | tf_op jit(solution)/shard_map/ppermute | solution.py:570
  139.6 5.3 %collective-permute-start.27 = (bf16[2,192,128]{2,1,0:T(8,128)(2,1)S(1)}, bf16[2,192,128]{2,1,0:T(8,128)(2,1)S(1)}, u32[]{:S(2)}, u32[]{:S(2)}) collective-permute-start(bf16[2,192,128]{2,1,0:T(8,128)(2,1)S(1)} %get-tuple-element.151), channel_id=1, source_target_pairs={{0,2},{2,0},{4,6},{6,4},{8,10},{10,8},{12,14},{14,12},{16,18},{18,... | collective-permute-start | bytes 294920 | tf_op jit(solution)/shard_map/ppermute | solution.py:570
  (29 other events, 190.3 us)

commit v2 on v1

--- a/solution.py
+++ b/solution.py
@@ -143,7 +143,7 @@
         input_output_aliases={8 + i: i for i in range(len(filled))},
         compiler_params=pltpu.CompilerParams(vmem_limit_bytes=VMEM),
         cost_estimate=pl.CostEstimate(
-            flops=(14000 if filled else 56000) * tokens * own, bytes_accessed=16 * tokens * own, transcendentals=0
+            flops=(14000 if filled else 28000) * tokens * own, bytes_accessed=16 * tokens * own, transcendentals=0
         ),
         name="hyena",
     )(*streams, inner, outer, short_filter, long_filter, *filled)
@@ -624,7 +624,7 @@
         coming = up(columns[-1])
         if hop == reach - 1:
             inner, columns[-1] = lax.optimization_barrier((inner, columns[-1]))
-            hyena_outs = hyena(streams, inner, outer, *filters, 0, 1)
+            hyena_outs = hyena(streams, inner, outer, *filters, 0, 2)
             coming, first_out = lax.optimization_barrier((coming, hyena_outs[0]))
             hyena_outs = [first_out] + list(hyena_outs[1:])
         columns.append(coming)
@@ -673,7 +673,7 @@
         coming = down(running)
         if back >= reach - 2:
             inner, running = lax.optimization_barrier((inner, running))
-            eighths = (1, 4) if back == reach - 1 else (5, 3)
+            eighths = (2, 4) if back == reach - 1 else (6, 2)
             hyena_outs = hyena(streams, inner, outer, *filters, *eighths, hyena_outs)
             coming, first_out = lax.optimization_barrier((coming, hyena_outs[0]))
             hyena_outs = [first_out] + list(hyena_outs[1:])

time: 148 us -> 144 us (0.973); the launches traced: 146 us -> 144 us
  Pallas kernels: 54.6 us -> 59.5 us
  waiting for transfers between devices: 38.9 us -> 34.5 us
  local copies, waits for them, and re-layouts: 9.91 us -> 8.35 us
    ppermute x2, waiting for transfers between devices: 12.7 us -> 23.4 us  [down(): return permute(values, perm=[(i + PLANE, i) for i in range(ctx - PLANE)])]
    ppermute x1, waiting for transfers between devices: 10.7 us -> 0.01 us  [body(): tail_term = permute(terms[0], perm=[(j, i) for i, j in far_pairs])]
    pallas_call x2, Pallas kernels: 25.8 us -> 30.6 us  [attention(): pl.pallas_call(functools.partial(attention_kernel, pieces, distances, gro...]
    ppermute x14, waiting for transfers between devices: 5.29 us -> 2.72 us  [exchange(): values[distance] = lax.ppermute(values[distance], ('ctx', 'tp'), perm)]
    unnamed x66 -> x64, local copies, waits for them, and re-layouts: 8.1 us -> 6.54 us
  transfers between devices with their start and end apart: 28 -> 28, of which waited for: 10 -> 7; matrix products, arithmetic and copies ran while one was open for 2% -> 2% of each run, Pallas kernels for 35% -> 38%
where the time goes in v2:
time: 144 us
  Pallas kernels  59.5 us (41%)
  starting transfers between devices  37.4 us (26%)
  waiting for transfers between devices  34.5 us (24%)
  local copies, waits for them, and re-layouts  8.35 us (6%)
  other arithmetic  2.76 us (2%)
    pallas_call x2, Pallas kernels, attention(): pl.pallas_call(functools.partial(attention_kernel, pieces, distances, gro...  30.6 us
    ppermute x2, waiting for transfers between devices, down(): return permute(values, perm=[(i + PLANE, i) for i in range(ctx - PLANE)])  23.4 us
    ppermute x14, starting transfers between devices, exchange(): values[distance] = lax.ppermute(values[distance], ('ctx', 'tp'), perm)  18.4 us
    pallas_call x3, Pallas kernels, hyena(): pl.pallas_call(functools.partial(hyena_kernel, first * width), grid=(step...  17.5 us
    unnamed x64, local copies, waits for them, and re-layouts  6.54 us
    ppermute x1, starting transfers between devices, body(): tail_kv = permute(tail_kv, perm=far_pairs)  6.3 us
    ppermute x6, waiting for transfers between devices, swap(): return permute(values, perm=[(i, i ^ distance) for i in range(ctx)])  5.34 us
    ppermute x2, starting transfers between devices, up(): return permute(values, perm=[(i, i + PLANE) for i in range(ctx - PLANE)])  4.81 us
  transfers between devices with their start and end apart: 28, of which 7 were waited for; matrix products, arithmetic and copies ran while one was open for 2% of the time, Pallas kernels for 38%

profile of v2, /device:TPU:0, one launch (start us, length us, event | category | flops | bytes accessed | tf_op | source)
XLA Modules:
  0.0 143.6 jit_solution(18334242757859693343)
XLA Ops:
  0.6 2.4 %pack_edges.1 = (bf16[2,96,128]{2,1,0:T(8,128)(2,1)}, bf16[2,96,128]{2,1,0:T(8,128)(2,1)}, bf16[2,96,128]{2,1,0:T(8,128)(2,1)}, bf16[2,96,128]{2,1,0:T(8,128)(2,...) custom-call(bf16[96,1024]{1,0:T(8,128)(2,1)} %k_ref.1, ...), custom_call_target="tpu_custom_call" | custom-call | tf_op jit(solution)/shard_map/pack_edges/pallas_call | solution.py:189
  3.1 3.3 %collective-permute-start.10 = (bf16[2,96,128]{2,1,0:T(8,128)(2,1)}, bf16[2,96,128]{2,1,0:T(8,128)(2,1)S(1)}, u32[]{:S(2)}, u32[]{:S(2)}) collective-permute-start(bf16[2,96,128]{2,1,0:T(8,128)(2,1)} %get-tuple-element.91), channel_id=1, source_target_pairs={{0,7},{2,5},{4,3},{6,1},{8,15},{10,13},{12,11},{14,9},{16,23},{18,... | collective-permute-start | bytes 147464 | tf_op jit(solution)/shard_map/ppermute | solution.py:592
  9.0 1.9 %collective-permute-start.8 = (bf16[2,96,128]{2,1,0:T(8,128)(2,1)}, bf16[2,96,128]{2,1,0:T(8,128)(2,1)}, u32[]{:S(2)}, u32[]{:S(2)}) collective-permute-start(bf16[2,96,128]{2,1,0:T(8,128)(2,1)} %get-tuple-element.89), channel_id=1, source_target_pairs={{0,3},{2,1},{4,7},{6,5},{8,11},{10,9},{12,15},{14,13},{16,19},{18,... | collective-permute-start | bytes 147464 | tf_op jit(solution)/shard_map/ppermute | solution.py:592
  10.9 1.4 collective-permute-start.9
  12.3 3.8 %pack_rows.1 = (bf16[96,2048]{1,0:T(8,128)(2,1)}, bf16[96,2048]{1,0:T(8,128)(2,1)}, bf16[96,2048]{1,0:T(8,128)(2,1)}, bf16[96,2048]{1,0:T(8,128)(2,1)}, bf16[96,...) custom-call(bf16[96,8192]{1,0:T(8,128)(2,1)} %q_ref, ...), custom_call_target="tpu_custom_call" | custom-call | tf_op jit(solution)/shard_map/pack_rows/pallas_call | solution.py:242
  16.8 1.8 %join.1.refs_7_ = bf16[2,768,128]{2,1,0:T(8,128)(2,1)} custom-call(bf16[2,96,128]{2,1,0:T(8,128)(2,1)} %get-tuple-element.84.refs_0_, bf16[2,96,128]{2,1,0:T(8,128)(2,1)} %copy-done.24, bf16[2,96,128]{2,1,0:T(8,128)(2,1)} %copy-done.25, bf16[2,96,128]{2,1,0:T(8,128)(2,1)} %copy-done.26, bf16[2,96,128]{2,1,0:T(8,128)(2,1)} %copy-done.27, ...), custom_call_target="tpu_custom_call" | custom-call | tf_op jit(solution)/shard_map/join/pallas_call | solution.py:213
  18.6 3.5 %collective-permute-start.12 = (bf16[2,768,128]{2,1,0:T(8,128)(2,1)}, bf16[2,768,128]{2,1,0:T(8,128)(2,1)S(1)}, u32[]{:S(2)}, u32[]{:S(2)}) collective-permute-start(bf16[2,768,128]{2,1,0:T(8,128)(2,1)} %join.1.refs_7_), channel_id=1, source_target_pairs={{0,8},{2,10},{4,12},{6,14},{8,16},{10,18},{12,20},{14,22},{16,24},... | collective-permute-start | bytes 1179656 | tf_op jit(solution)/shard_map/ppermute | solution.py:564
  23.9 4.0 %collective-permute-start.16 = (bf16[96,2048]{1,0:T(8,128)(2,1)}, bf16[96,2048]{1,0:T(8,128)(2,1)S(1)}, u32[]{:S(2)}, u32[]{:S(2)}) collective-permute-start(bf16[96,2048]{1,0:T(8,128)(2,1)} %get-tuple-element.104), channel_id=1, source_target_pairs={{0,6},{2,4},{4,2},{6,0},{8,14},{10,12},{12,10},{14,8},{16,22},{18,... | collective-permute-start | bytes 1179656 | tf_op jit(solution)/shard_map/ppermute | solution.py:592
  27.9 1.0 collective-permute-start.17
  29.4 1.7 %collective-permute-done.12.refs_8_ = bf16[2,768,128]{2,1,0:T(8,128)(2,1)S(1)} collective-permute-done((bf16[2,768,128]{2,1,0:T(8,128)(2,1)}, bf16[2,768,128]{2,1,0:T(8,128)(2,1)S(1)}, u32[]{:S(2)}, u32[]{:S(2)}) %collective-permute-start.12) | collective-permute-done | bytes 393248 | tf_op jit(solution)/shard_map/ppermute | solution.py:564
  31.1 6.3 %collective-permute-start.13 = (bf16[2,192,128]{2,1,0:T(8,128)(2,1)S(1)}, bf16[2,192,128]{2,1,0:T(8,128)(2,1)S(1)}, u32[]{:S(2)}, u32[]{:S(2)}) collective-permute-start(bf16[2,192,128]{2,1,0:T(8,128)(2,1)S(1)} %slice.16), channel_id=1, source_target_pairs={{0,24},{2,26},{4,28},{6,30},{1,25},{3,27},{5,29},{7,31}} | collective-permute-start | bytes 294920 | tf_op jit(solution)/shard_map/ppermute | solution.py:633
  37.4 1.3 collective-permute-start.14
  38.8 1.4 copy-done.1
  40.2 1.4 copy-done.4
  41.6 4.9 %hyena.3 = (bf16[192,4096]{1,0:T(8,128)(2,1)}, bf16[192,4096]{1,0:T(8,128)(2,1)}, bf16[192,4096]{1,0:T(8,128)(2,1)}, bf16[192,4096]{1,0:T(8,128)(2,1)}) custom-call(bf16[192,4096]{1,0:T(8,128)(2,1)S(1)} %copy-done, bf16[192,4096]{1,0:T(8,128)(2,1)S(1)} %copy-done.1, bf16[192,4096]{1,0:T(8,128)(2,1)S(1)} %copy-done.4, bf16[192,4096]{1,0:T(8,128)(2,1)} %grad_ref.5, ...), custom_call_target="tpu_custom_call" | custom-call | flops 5505024000 | bytes 3145728 | tf_op jit(solution)/shard_map/hyena/pallas_call | solution.py:127
  46.5 1.4 %collective-permute-done.14.refs_9_ = bf16[2,768,128]{2,1,0:T(8,128)(2,1)S(1)} collective-permute-done((bf16[2,768,128]{2,1,0:T(8,128)(2,1)S(1)}, bf16[2,768,128]{2,1,0:T(8,128)(2,1)S(1)}, u32[]{:S(2)}, u32[]{:S(2)}) %collective-permute-start.14) | collective-permute-done | bytes 393248 | tf_op jit(solution)/shard_map/ppermute | solution.py:564
  48.3 2.6 %collective-permute-start.1 = (bf16[96,2048]{1,0:T(8,128)(2,1)S(1)}, bf16[96,2048]{1,0:T(8,128)(2,1)S(1)}, u32[]{:S(2)}, u32[]{:S(2)}) collective-permute-start(bf16[96,2048]{1,0:T(8,128)(2,1)S(1)} %copy-done.30), channel_id=1, source_target_pairs={{0,5},{2,7},{4,1},{6,3},{8,13},{10,15},{12,9},{14,11},{16,21},{18,... | collective-permute-start | bytes 1179656 | tf_op jit(solution)/shard_map/ppermute | solution.py:592
  52.6 14.6 %attention.2 = (bf16[192,2048]{1,0:T(8,128)(2,1)S(1)}, bf16[192,2048]{1,0:T(8,128)(2,1)S(1)}, bf16[2,192,128]{2,1,0:T(8,128)(2,1)S(1)}, bf16[2,768,128]{2,1,0:T(...) custom-call(s32[5]{0:T(128)S(1)} %stack.10.refs_0_, s32[16]{0:T(128)S(1)} %copy-done.22, ...), custom_call_target="tpu_custom_call" | custom-call | flops 48318382080 | bytes 12582912 | tf_op jit(solution)/shard_map/attention/pallas_call | solution.py:452
  67.7 2.6 %collective-permute-done.3.refs_5_ = bf16[96,2048]{1,0:T(8,128)(2,1)S(1)} collective-permute-done((bf16[96,2048]{1,0:T(8,128)(2,1)S(1)}, bf16[96,2048]{1,0:T(8,128)(2,1)S(1)}, u32[]{:S(2)}, u32[]{:S(2)}) %collective-permute-start.3) | collective-permute-done | bytes 393248 | tf_op jit(solution)/shard_map/ppermute | solution.py:592
  70.3 15.9 %attention.3 = (bf16[192,2048]{1,0:T(8,128)(2,1)}, bf16[192,2048]{1,0:T(8,128)(2,1)}, bf16[2,192,128]{2,1,0:T(8,128)(2,1)S(1)}, bf16[2,768,128]{2,1,0:T(8,128)(2...) custom-call(s32[5]{0:T(128)S(1)} %stack.10.refs_0_, s32[16]{0:T(128)S(1)} %copy-done.22, ...), custom_call_target="tpu_custom_call" | custom-call | flops 48318382080 | bytes 12582912 | tf_op jit(solution)/shard_map/attention/pallas_call | solution.py:452
  87.3 1.3 collective-permute-start.20
  88.6 7.7 %hyena.4 = (bf16[192,4096]{1,0:T(8,128)(2,1)}, bf16[192,4096]{1,0:T(8,128)(2,1)}, bf16[192,4096]{1,0:T(8,128)(2,1)}, bf16[192,4096]{1,0:T(8,128)(2,1)}) custom-call(bf16[192,4096]{1,0:T(8,128)(2,1)S(1)} %copy-done, bf16[192,4096]{1,0:T(8,128)(2,1)S(1)} %copy-done.2, ...), custom_call_target="tpu_custom_call", output_to_operand_aliasing={{0}: (8, {}), {1}: (9, {}), {2}: (10, {}), {3}: (11, {})} | custom-call | flops 5505024000 | bytes 6291456 | tf_op jit(solution)/shard_map/hyena/pallas_call | solution.py:127
  96.3 22.9 %collective-permute-done.20 = bf16[2,768,128]{2,1,0:T(8,128)(2,1)S(1)} collective-permute-done((bf16[2,768,128]{2,1,0:T(8,128)(2,1)S(1)}, bf16[2,768,128]{2,1,0:T(8,128)(2,1)S(1)}, u32[]{:S(2)}, u32[]{:S(2)}) %collective-permute-start.20) | collective-permute-done | bytes 393248 | tf_op jit(solution)/shard_map/ppermute | solution.py:567
  120.1 1.3 collective-permute-start.21
  121.4 1.3 collective-permute-start.24
  122.7 1.1 copy-done.8
  123.8 3.4 %settle.1 = (bf16[192,4096]{1,0:T(8,128)(2,1)}, bf16[192,4096]{1,0:T(8,128)(2,1)}) custom-call(bf16[192,2048]{1,0:T(8,128)(2,1)S(1)} %get-tuple-element.131.refs_0_, bf16[192,2048]{1,0:T(8,128)(2,1)} %collective-permute-done.22.refs_1_, bf16[192,2048]{1,0:T(8,128)(2,1)} %collective-permute-done.23.refs_2_, bf16[192,2048]{1,0:T(8,128)(2,1)S(1)} %copy-done.8), custom_call_target="tpu_custom_call" | custom-call | tf_op jit(solution)/shard_map/settle/pallas_call | solution.py:505
  128.2 4.9 %hyena.5 = (bf16[192,4096]{1,0:T(8,128)(2,1)}, bf16[192,4096]{1,0:T(8,128)(2,1)}, bf16[192,4096]{1,0:T(8,128)(2,1)}, bf16[192,4096]{1,0:T(8,128)(2,1)}) custom-call(bf16[192,4096]{1,0:T(8,128)(2,1)S(1)} %copy-done, bf16[192,4096]{1,0:T(8,128)(2,1)S(1)} %copy-done.3, ...), custom_call_target="tpu_custom_call", output_to_operand_aliasing={{0}: (8, {}), {1}: (9, {}), {2}: (10, {}), {3}: (11, {})} | custom-call | flops 2752512000 | bytes 3145728 | tf_op jit(solution)/shard_map/hyena/pallas_call | solution.py:127
  133.6 1.1 convert_add_fusion
  135.4 1.7 %collective-permute-start.26 = (bf16[2,192,128]{2,1,0:T(8,128)(2,1)S(1)}, bf16[2,192,128]{2,1,0:T(8,128)(2,1)S(1)}, u32[]{:S(2)}, u32[]{:S(2)}) collective-permute-start(bf16[2,192,128]{2,1,0:T(8,128)(2,1)S(1)} %get-tuple-element.153), channel_id=1, source_target_pairs={{0,4},{2,6},{4,0},{6,2},{8,12},{10,14},{12,8},{14,10},{16,20},{18,... | collective-permute-start | bytes 294920 | tf_op jit(solution)/shard_map/ppermute | solution.py:570
  137.2 3.0 %collective-permute-done.25 = bf16[2,192,128]{2,1,0:T(8,128)(2,1)S(1)} collective-permute-done((bf16[2,192,128]{2,1,0:T(8,128)(2,1)S(1)}, bf16[2,192,128]{2,1,0:T(8,128)(2,1)S(1)}, u32[]{:S(2)}, u32[]{:S(2)}) %collective-permute-start.25) | collective-permute-done | bytes 98336 | tf_op jit(solution)/shard_map/ppermute | solution.py:570
  140.3 2.3 %collective-permute-done.26 = bf16[2,192,128]{2,1,0:T(8,128)(2,1)S(1)} collective-permute-done((bf16[2,192,128]{2,1,0:T(8,128)(2,1)S(1)}, bf16[2,192,128]{2,1,0:T(8,128)(2,1)S(1)}, u32[]{:S(2)}, u32[]{:S(2)}) %collective-permute-start.26) | collective-permute-done | bytes 98336 | tf_op jit(solution)/shard_map/ppermute | solution.py:570
  (108 shorter events, 13.1 us)
Async XLA Ops:
  3.1 5.9 %collective-permute-start.10 = (bf16[2,96,128]{2,1,0:T(8,128)(2,1)}, bf16[2,96,128]{2,1,0:T(8,128)(2,1)S(1)}, u32[]{:S(2)}, u32[]{:S(2)}) collective-permute-start(bf16[2,96,128]{2,1,0:T(8,128)(2,1)} %get-tuple-element.91), channel_id=1, source_target_pairs={{0,7},{2,5},{4,3},{6,1},{8,15},{10,13},{12,11},{14,9},{16,23},{18,... | collective-permute-start | bytes 147464 | tf_op jit(solution)/shard_map/ppermute | solution.py:592
  6.4 4.5 %collective-permute-start.4 = (bf16[2,96,128]{2,1,0:T(8,128)(2,1)}, bf16[2,96,128]{2,1,0:T(8,128)(2,1)S(1)}, u32[]{:S(2)}, u32[]{:S(2)}) collective-permute-start(bf16[2,96,128]{2,1,0:T(8,128)(2,1)} %get-tuple-element.85), channel_id=1, source_target_pairs={{0,2},{2,0},{4,6},{6,4},{8,10},{10,8},{12,14},{14,12},{16,18},{18,... | collective-permute-start | bytes 147464 | tf_op jit(solution)/shard_map/ppermute | solution.py:592
  7.1 9.1 %collective-permute-start.5 = (bf16[2,96,128]{2,1,0:T(8,128)(2,1)}, bf16[2,96,128]{2,1,0:T(8,128)(2,1)S(1)}, u32[]{:S(2)}, u32[]{:S(2)}) collective-permute-start(bf16[2,96,128]{2,1,0:T(8,128)(2,1)} %get-tuple-element.86), channel_id=1, source_target_pairs={{0,4},{2,6},{4,0},{6,2},{8,12},{10,14},{12,8},{14,10},{16,20},{18,... | collective-permute-start | bytes 147464 | tf_op jit(solution)/shard_map/ppermute | solution.py:592
  7.6 8.6 %collective-permute-start.6 = (bf16[2,96,128]{2,1,0:T(8,128)(2,1)}, bf16[2,96,128]{2,1,0:T(8,128)(2,1)S(1)}, u32[]{:S(2)}, u32[]{:S(2)}) collective-permute-start(bf16[2,96,128]{2,1,0:T(8,128)(2,1)} %get-tuple-element.87), channel_id=1, source_target_pairs={{0,6},{2,4},{4,2},{6,0},{8,14},{10,12},{12,10},{14,8},{16,22},{18,... | collective-permute-start | bytes 147464 | tf_op jit(solution)/shard_map/ppermute | solution.py:592
  8.4 7.8 %collective-permute-start.7 = (bf16[2,96,128]{2,1,0:T(8,128)(2,1)}, bf16[2,96,128]{2,1,0:T(8,128)(2,1)S(1)}, u32[]{:S(2)}, u32[]{:S(2)}) collective-permute-start(bf16[2,96,128]{2,1,0:T(8,128)(2,1)} %get-tuple-element.88), channel_id=1, source_target_pairs={{0,1},{2,3},{4,5},{6,7},{8,9},{10,11},{12,13},{14,15},{16,17},{18,... | collective-permute-start | bytes 147464 | tf_op jit(solution)/shard_map/ppermute | solution.py:592
  9.0 7.3 %collective-permute-start.8 = (bf16[2,96,128]{2,1,0:T(8,128)(2,1)}, bf16[2,96,128]{2,1,0:T(8,128)(2,1)}, u32[]{:S(2)}, u32[]{:S(2)}) collective-permute-start(bf16[2,96,128]{2,1,0:T(8,128)(2,1)} %get-tuple-element.89), channel_id=1, source_target_pairs={{0,3},{2,1},{4,7},{6,5},{8,11},{10,9},{12,15},{14,13},{16,19},{18,... | collective-permute-start | bytes 147464 | tf_op jit(solution)/shard_map/ppermute | solution.py:592
  10.9 5.3 %collective-permute-start.9 = (bf16[2,96,128]{2,1,0:T(8,128)(2,1)}, bf16[2,96,128]{2,1,0:T(8,128)(2,1)}, u32[]{:S(2)}, u32[]{:S(2)}) collective-permute-start(bf16[2,96,128]{2,1,0:T(8,128)(2,1)} %get-tuple-element.90), channel_id=1, source_target_pairs={{0,5},{2,7},{4,1},{6,3},{8,13},{10,15},{12,9},{14,11},{16,21},{18,... | collective-permute-start | bytes 147464 | tf_op jit(solution)/shard_map/ppermute | solution.py:592
  12.3 26.4 %copy-start.13 = (f32[3,3,4096]{2,1,0:T(4,128)S(1)}, f32[3,3,4096]{2,1,0:T(4,128)}, u32[]{:S(2)}) copy-start(f32[3,3,4096]{2,1,0:T(4,128)} %short_ref.5) | copy-start | bytes 442372
  12.3 26.4 %copy-start.16 = (f32[7,256]{1,0:T(8,128)S(1)}, f32[7,256]{1,0:T(8,128)}, u32[]{:S(2)}) copy-start(f32[7,256]{1,0:T(8,128)} %long_ref.5) | copy-start | bytes 21508
  18.6 12.5 %collective-permute-start.12 = (bf16[2,768,128]{2,1,0:T(8,128)(2,1)}, bf16[2,768,128]{2,1,0:T(8,128)(2,1)S(1)}, u32[]{:S(2)}, u32[]{:S(2)}) collective-permute-start(bf16[2,768,128]{2,1,0:T(8,128)(2,1)} %join.1.refs_7_), channel_id=1, source_target_pairs={{0,8},{2,10},{4,12},{6,14},{8,16},{10,18},{12,20},{14,22},{16,24},... | collective-permute-start | bytes 1179656 | tf_op jit(solution)/shard_map/ppermute | solution.py:564
  22.1 6.8 %collective-permute-start.11 = (bf16[32,4096]{1,0:T(8,128)(2,1)}, bf16[32,4096]{1,0:T(8,128)(2,1)S(1)}, u32[]{:S(2)}, u32[]{:S(2)}) collective-permute-start(bf16[32,4096]{1,0:T(8,128)(2,1)} %get-tuple-element.96), channel_id=1, source_target_pairs={{0,2},{2,0},{4,6},{6,4},{8,10},{10,8},{12,14},{14,12},{16,18},{18,... | collective-permute-start | bytes 786440 | tf_op jit(solution)/shard_map/ppermute | solution.py:579
  22.2 15.2 %collective-permute-start.15 = (bf16[32,4096]{1,0:T(8,128)(2,1)}, bf16[32,4096]{1,0:T(8,128)(2,1)S(1)}, u32[]{:S(2)}, u32[]{:S(2)}) collective-permute-start(bf16[32,4096]{1,0:T(8,128)(2,1)} %get-tuple-element.101), channel_id=1, source_target_pairs={{2,4},{4,2},{6,8},{8,6},{10,12},{12,10},{14,16},{16,14},{18,20},{2... | collective-permute-start | bytes 786440 | tf_op jit(solution)/shard_map/ppermute | solution.py:580
  23.0 28.6 %copy-start.22 = (s32[16]{0:T(128)S(1)}, s32[16]{0:T(128)}, u32[]{:S(2)}) copy-start(s32[16]{0:T(128)} %refs_1_.5) | copy-start | bytes 196
  23.9 24.4 %collective-permute-start.16 = (bf16[96,2048]{1,0:T(8,128)(2,1)}, bf16[96,2048]{1,0:T(8,128)(2,1)S(1)}, u32[]{:S(2)}, u32[]{:S(2)}) collective-permute-start(bf16[96,2048]{1,0:T(8,128)(2,1)} %get-tuple-element.104), channel_id=1, source_target_pairs={{0,6},{2,4},{4,2},{6,0},{8,14},{10,12},{12,10},{14,8},{16,22},{18,... | collective-permute-start | bytes 1179656 | tf_op jit(solution)/shard_map/ppermute | solution.py:592
  27.9 23.0 %collective-permute-start.17 = (bf16[96,2048]{1,0:T(8,128)(2,1)}, bf16[96,2048]{1,0:T(8,128)(2,1)S(1)}, u32[]{:S(2)}, u32[]{:S(2)}) collective-permute-start(bf16[96,2048]{1,0:T(8,128)(2,1)} %get-tuple-element.105), channel_id=1, source_target_pairs={{0,7},{2,5},{4,3},{6,1},{8,15},{10,13},{12,11},{14,9},{16,23},{18,... | collective-permute-start | bytes 1179656 | tf_op jit(solution)/shard_map/ppermute | solution.py:592
  28.9 22.0 %collective-permute-start.18 = (bf16[96,2048]{1,0:T(8,128)(2,1)}, bf16[96,2048]{1,0:T(8,128)(2,1)S(1)}, u32[]{:S(2)}, u32[]{:S(2)}) collective-permute-start(bf16[96,2048]{1,0:T(8,128)(2,1)} %get-tuple-element.107), channel_id=1, source_target_pairs={{0,1},{2,3},{4,5},{6,7},{8,9},{10,11},{12,13},{14,15},{16,17},{18,... | collective-permute-start | bytes 1179656 | tf_op jit(solution)/shard_map/ppermute | solution.py:592
  31.1 20.5 %collective-permute-start.13 = (bf16[2,192,128]{2,1,0:T(8,128)(2,1)S(1)}, bf16[2,192,128]{2,1,0:T(8,128)(2,1)S(1)}, u32[]{:S(2)}, u32[]{:S(2)}) collective-permute-start(bf16[2,192,128]{2,1,0:T(8,128)(2,1)S(1)} %slice.16), channel_id=1, source_target_pairs={{0,24},{2,26},{4,28},{6,30},{1,25},{3,27},{5,29},{7,31}} | collective-permute-start | bytes 294920 | tf_op jit(solution)/shard_map/ppermute | solution.py:633
  37.4 10.5 %collective-permute-start.14 = (bf16[2,768,128]{2,1,0:T(8,128)(2,1)S(1)}, bf16[2,768,128]{2,1,0:T(8,128)(2,1)S(1)}, u32[]{:S(2)}, u32[]{:S(2)}) collective-permute-start(bf16[2,768,128]{2,1,0:T(8,128)(2,1)S(1)} %collective-permute-done.12.refs_8_), channel_id=1, source_target_pairs={{0,8},{2,10},{4,12},{6,14},{8,16},{10,18},{12,20},{14,22},{16,24},... | collective-permute-start | bytes 1179656 | tf_op jit(solution)/shard_map/ppermute | solution.py:564
  47.9 19.7 %collective-permute-start = (bf16[96,2048]{1,0:T(8,128)(2,1)S(1)}, bf16[96,2048]{1,0:T(8,128)(2,1)S(1)}, u32[]{:S(2)}, u32[]{:S(2)}) collective-permute-start(bf16[96,2048]{1,0:T(8,128)(2,1)S(1)} %copy-done.31), channel_id=1, source_target_pairs={{0,4},{2,6},{4,0},{6,2},{8,12},{10,14},{12,8},{14,10},{16,20},{18,... | collective-permute-start | bytes 1179656 | tf_op jit(solution)/shard_map/ppermute | solution.py:592
  48.3 19.3 %collective-permute-start.1 = (bf16[96,2048]{1,0:T(8,128)(2,1)S(1)}, bf16[96,2048]{1,0:T(8,128)(2,1)S(1)}, u32[]{:S(2)}, u32[]{:S(2)}) collective-permute-start(bf16[96,2048]{1,0:T(8,128)(2,1)S(1)} %copy-done.30), channel_id=1, source_target_pairs={{0,5},{2,7},{4,1},{6,3},{8,13},{10,15},{12,9},{14,11},{16,21},{18,... | collective-permute-start | bytes 1179656 | tf_op jit(solution)/shard_map/ppermute | solution.py:592
  50.9 16.7 %collective-permute-start.2 = (bf16[96,2048]{1,0:T(8,128)(2,1)S(1)}, bf16[96,2048]{1,0:T(8,128)(2,1)S(1)}, u32[]{:S(2)}, u32[]{:S(2)}) collective-permute-start(bf16[96,2048]{1,0:T(8,128)(2,1)S(1)} %copy-done.29), channel_id=1, source_target_pairs={{0,2},{2,0},{4,6},{6,4},{8,10},{10,8},{12,14},{14,12},{16,18},{18,... | collective-permute-start | bytes 1179656 | tf_op jit(solution)/shard_map/ppermute | solution.py:592
  51.0 19.3 %collective-permute-start.3 = (bf16[96,2048]{1,0:T(8,128)(2,1)S(1)}, bf16[96,2048]{1,0:T(8,128)(2,1)S(1)}, u32[]{:S(2)}, u32[]{:S(2)}) collective-permute-start(bf16[96,2048]{1,0:T(8,128)(2,1)S(1)} %copy-done.28), channel_id=1, source_target_pairs={{0,3},{2,1},{4,7},{6,5},{8,11},{10,9},{12,15},{14,13},{16,19},{18,... | collective-permute-start | bytes 1179656 | tf_op jit(solution)/shard_map/ppermute | solution.py:592
  67.2 20.0 %collective-permute-start.19 = (bf16[192,2048]{1,0:T(8,128)(2,1)S(1)}, bf16[192,2048]{1,0:T(8,128)(2,1)S(1)}, u32[]{:S(2)}, u32[]{:S(2)}) collective-permute-start(bf16[192,2048]{1,0:T(8,128)(2,1)S(1)} %get-tuple-element.114), channel_id=1, source_target_pairs={{0,6},{2,4},{4,2},{6,0},{8,14},{10,12},{12,10},{14,8},{16,22},{18,... | collective-permute-start | bytes 2359304 | tf_op jit(solution)/shard_map/ppermute | solution.py:570
  86.3 36.4 %collective-permute-start.22 = (bf16[192,2048]{1,0:T(8,128)(2,1)}, bf16[192,2048]{1,0:T(8,128)(2,1)}, u32[]{:S(2)}, u32[]{:S(2)}) collective-permute-start(bf16[192,2048]{1,0:T(8,128)(2,1)} %get-tuple-element.132), channel_id=1, source_target_pairs={{0,2},{2,0},{4,6},{6,4},{8,10},{10,8},{12,14},{14,12},{16,18},{18,... | collective-permute-start | bytes 2359304 | tf_op jit(solution)/shard_map/ppermute | solution.py:570
  86.9 35.8 %collective-permute-start.23 = (bf16[192,2048]{1,0:T(8,128)(2,1)}, bf16[192,2048]{1,0:T(8,128)(2,1)}, u32[]{:S(2)}, u32[]{:S(2)}) collective-permute-start(bf16[192,2048]{1,0:T(8,128)(2,1)} %get-tuple-element.133), channel_id=1, source_target_pairs={{0,4},{2,6},{4,0},{6,2},{8,12},{10,14},{12,8},{14,10},{16,20},{18,... | collective-permute-start | bytes 2359304 | tf_op jit(solution)/shard_map/ppermute | solution.py:570
  87.3 31.9 %collective-permute-start.20 = (bf16[2,768,128]{2,1,0:T(8,128)(2,1)S(1)}, bf16[2,768,128]{2,1,0:T(8,128)(2,1)S(1)}, u32[]{:S(2)}, u32[]{:S(2)}) collective-permute-start(bf16[2,768,128]{2,1,0:T(8,128)(2,1)S(1)} %get-tuple-element.116), channel_id=1, source_target_pairs={{8,0},{10,2},{12,4},{14,6},{16,8},{18,10},{20,12},{22,14},{24,16},... | collective-permute-start | bytes 1179656 | tf_op jit(solution)/shard_map/ppermute | solution.py:567
  88.6 38.6 %copy-start.12 = (bf16[32,4096]{1,0:T(8,128)(2,1)S(1)}, bf16[32,4096]{1,0:T(8,128)(2,1)}, u32[]{:S(2)}) copy-start(bf16[32,4096]{1,0:T(8,128)(2,1)} %copy-done.10) | copy-start | bytes 786436
  120.1 13.5 %collective-permute-start.21 = (bf16[2,768,128]{2,1,0:T(8,128)(2,1)}, bf16[2,768,128]{2,1,0:T(8,128)(2,1)}, u32[]{:S(2)}, u32[]{:S(2)}) collective-permute-start(bf16[2,768,128]{2,1,0:T(8,128)(2,1)} %add_convert_fusion), channel_id=1, source_target_pairs={{8,0},{10,2},{12,4},{14,6},{16,8},{18,10},{20,12},{22,14},{24,16},... | collective-permute-start | bytes 1179656 | tf_op jit(solution)/shard_map/ppermute | solution.py:567
  121.4 13.3 %collective-permute-start.24 = (bf16[2,192,128]{2,1,0:T(8,128)(2,1)}, bf16[2,192,128]{2,1,0:T(8,128)(2,1)S(1)}, u32[]{:S(2)}, u32[]{:S(2)}) collective-permute-start(bf16[2,192,128]{2,1,0:T(8,128)(2,1)} %copy-done.21), channel_id=1, source_target_pairs={{24,0},{26,2},{28,4},{30,6},{25,1},{27,3},{29,5},{31,7}} | collective-permute-start | bytes 294920 | tf_op jit(solution)/shard_map/ppermute | solution.py:670
  135.3 5.0 %collective-permute-start.25 = (bf16[2,192,128]{2,1,0:T(8,128)(2,1)S(1)}, bf16[2,192,128]{2,1,0:T(8,128)(2,1)S(1)}, u32[]{:S(2)}, u32[]{:S(2)}) collective-permute-start(bf16[2,192,128]{2,1,0:T(8,128)(2,1)S(1)} %get-tuple-element.152), channel_id=1, source_target_pairs={{0,6},{2,4},{4,2},{6,0},{8,14},{10,12},{12,10},{14,8},{16,22},{18,... | collective-permute-start | bytes 294920 | tf_op jit(solution)/shard_map/ppermute | solution.py:570
  135.4 7.2 %collective-permute-start.26 = (bf16[2,192,128]{2,1,0:T(8,128)(2,1)S(1)}, bf16[2,192,128]{2,1,0:T(8,128)(2,1)S(1)}, u32[]{:S(2)}, u32[]{:S(2)}) collective-permute-start(bf16[2,192,128]{2,1,0:T(8,128)(2,1)S(1)} %get-tuple-element.153), channel_id=1, source_target_pairs={{0,4},{2,6},{4,0},{6,2},{8,12},{10,14},{12,8},{14,10},{16,20},{18,... | collective-permute-start | bytes 294920 | tf_op jit(solution)/shard_map/ppermute | solution.py:570
  137.1 5.5 %collective-permute-start.27 = (bf16[2,192,128]{2,1,0:T(8,128)(2,1)S(1)}, bf16[2,192,128]{2,1,0:T(8,128)(2,1)S(1)}, u32[]{:S(2)}, u32[]{:S(2)}) collective-permute-start(bf16[2,192,128]{2,1,0:T(8,128)(2,1)S(1)} %get-tuple-element.151), channel_id=1, source_target_pairs={{0,2},{2,0},{4,6},{6,4},{8,10},{10,8},{12,14},{14,12},{16,18},{18,... | collective-permute-start | bytes 294920 | tf_op jit(solution)/shard_map/ppermute | solution.py:570
  (28 other events, 239.6 us)

commit v3 on v2

--- a/solution.py
+++ b/solution.py
@@ -143,7 +143,7 @@
         input_output_aliases={8 + i: i for i in range(len(filled))},
         compiler_params=pltpu.CompilerParams(vmem_limit_bytes=VMEM),
         cost_estimate=pl.CostEstimate(
-            flops=(14000 if filled else 28000) * tokens * own, bytes_accessed=16 * tokens * own, transcendentals=0
+            flops=14000 * tokens * own, bytes_accessed=16 * tokens * own, transcendentals=0
         ),
         name="hyena",
     )(*streams, inner, outer, short_filter, long_filter, *filled)
@@ -624,7 +624,7 @@
         coming = up(columns[-1])
         if hop == reach - 1:
             inner, columns[-1] = lax.optimization_barrier((inner, columns[-1]))
-            hyena_outs = hyena(streams, inner, outer, *filters, 0, 2)
+            hyena_outs = hyena(streams, inner, outer, *filters, 0, 4)
             coming, first_out = lax.optimization_barrier((coming, hyena_outs[0]))
             hyena_outs = [first_out] + list(hyena_outs[1:])
         columns.append(coming)
@@ -671,10 +671,9 @@
     running = plane_sum(reach).astype(bf16)
     for back in range(reach - 1, -1, -1):
         coming = down(running)
-        if back >= reach - 2:
+        if back == reach - 1:
             inner, running = lax.optimization_barrier((inner, running))
-            eighths = (2, 4) if back == reach - 1 else (6, 2)
-            hyena_outs = hyena(streams, inner, outer, *filters, *eighths, hyena_outs)
+            hyena_outs = hyena(streams, inner, outer, *filters, 4, 4, hyena_outs)
             coming, first_out = lax.optimization_barrier((coming, hyena_outs[0]))
             hyena_outs = [first_out] + list(hyena_outs[1:])
         running = plane_sum(back) + coming.astype(f32)

time: 144 us -> 146 us (1.014)
  waiting for transfers between devices: 34.5 us -> 42.5 us
  Pallas kernels: 59.5 us -> 52.5 us
  starting transfers between devices: 37.4 us -> 39.7 us
  other arithmetic: 2.76 us -> 1.03 us
    pallas_call x2, Pallas kernels: 30.6 us -> 25.5 us  [attention(): pl.pallas_call(functools.partial(attention_kernel, pieces, distances, gro...]
    ppermute x1, waiting for transfers between devices: 0.01 us -> 4.1 us  [body(): tail_term = permute(terms[0], perm=[(j, i) for i, j in far_pairs])]
    ppermute x14, waiting for transfers between devices: 2.72 us -> 6.15 us  [exchange(): values[distance] = lax.ppermute(values[distance], ('ctx', 'tp'), perm)]
    ppermute x2, waiting for transfers between devices: 23.4 us -> 25.7 us  [down(): return permute(values, perm=[(i + PLANE, i) for i in range(ctx - PLANE)])]
    ppermute x6, starting transfers between devices: 3.31 us -> 5.23 us  [swap(): return permute(values, perm=[(i, i ^ distance) for i in range(ctx)])]
    pallas_call x3 -> x2, Pallas kernels: 17.5 us -> 15.7 us  [hyena(): pl.pallas_call(functools.partial(hyena_kernel, first * width), grid=(step...]
    unnamed x64 -> x58, local copies, waits for them, and re-layouts: 6.54 us -> 6.03 us
  transfers between devices with their start and end apart: 28 -> 28, of which waited for: 7 -> 9; matrix products, arithmetic and copies ran while one was open for 2% -> 1% of each run, Pallas kernels for 38% -> 33%
where the time goes in v3:
time: 146 us; the launch traced here: 145 us
  Pallas kernels  52.5 us (36%)
  waiting for transfers between devices  42.5 us (29%)
  starting transfers between devices  39.7 us (27%)
  local copies, waits for them, and re-layouts  7.84 us (5%)
    ppermute x2, waiting for transfers between devices, down(): return permute(values, perm=[(i + PLANE, i) for i in range(ctx - PLANE)])  25.7 us
    pallas_call x2, Pallas kernels, attention(): pl.pallas_call(functools.partial(attention_kernel, pieces, distances, gro...  25.5 us
    ppermute x14, starting transfers between devices, exchange(): values[distance] = lax.ppermute(values[distance], ('ctx', 'tp'), perm)  18.4 us
    pallas_call x2, Pallas kernels, hyena(): pl.pallas_call(functools.partial(hyena_kernel, first * width), grid=(step...  15.7 us
    ppermute x1, starting transfers between devices, body(): tail_kv = permute(tail_kv, perm=far_pairs)  6.3 us
    ppermute x14, waiting for transfers between devices, exchange(): values[distance] = lax.ppermute(values[distance], ('ctx', 'tp'), perm)  6.15 us
    unnamed x58, local copies, waits for them, and re-layouts  6.03 us
    ppermute x6, starting transfers between devices, swap(): return permute(values, perm=[(i, i ^ distance) for i in range(ctx)])  5.23 us
  transfers between devices with their start and end apart: 28, of which 9 were waited for; matrix products, arithmetic and copies ran while one was open for 1% of the time, Pallas kernels for 33%

profile of v3, /device:TPU:0, one launch (start us, length us, event | category | flops | bytes accessed | tf_op | source)
XLA Modules:
  0.0 144.7 jit_solution(8128118370432874067)
XLA Ops:
  0.6 2.4 %pack_edges.1 = (bf16[2,96,128]{2,1,0:T(8,128)(2,1)}, bf16[2,96,128]{2,1,0:T(8,128)(2,1)}, bf16[2,96,128]{2,1,0:T(8,128)(2,1)}, bf16[2,96,128]{2,1,0:T(8,128)(2,...) custom-call(bf16[96,1024]{1,0:T(8,128)(2,1)} %k_ref.1, ...), custom_call_target="tpu_custom_call" | custom-call | tf_op jit(solution)/shard_map/pack_edges/pallas_call | solution.py:189
  3.1 3.3 %collective-permute-start.10 = (bf16[2,96,128]{2,1,0:T(8,128)(2,1)}, bf16[2,96,128]{2,1,0:T(8,128)(2,1)S(1)}, u32[]{:S(2)}, u32[]{:S(2)}) collective-permute-start(bf16[2,96,128]{2,1,0:T(8,128)(2,1)} %get-tuple-element.84), channel_id=1, source_target_pairs={{0,7},{2,5},{4,3},{6,1},{8,15},{10,13},{12,11},{14,9},{16,23},{18,... | collective-permute-start | bytes 147464 | tf_op jit(solution)/shard_map/ppermute | solution.py:592
  9.0 1.9 %collective-permute-start.8 = (bf16[2,96,128]{2,1,0:T(8,128)(2,1)}, bf16[2,96,128]{2,1,0:T(8,128)(2,1)S(1)}, u32[]{:S(2)}, u32[]{:S(2)}) collective-permute-start(bf16[2,96,128]{2,1,0:T(8,128)(2,1)} %get-tuple-element.82), channel_id=1, source_target_pairs={{0,3},{2,1},{4,7},{6,5},{8,11},{10,9},{12,15},{14,13},{16,19},{18,... | collective-permute-start | bytes 147464 | tf_op jit(solution)/shard_map/ppermute | solution.py:592
  10.9 1.4 collective-permute-start.9
  12.3 3.8 %pack_rows.1 = (bf16[96,2048]{1,0:T(8,128)(2,1)}, bf16[96,2048]{1,0:T(8,128)(2,1)}, bf16[96,2048]{1,0:T(8,128)(2,1)}, bf16[96,2048]{1,0:T(8,128)(2,1)}, bf16[96,...) custom-call(bf16[96,8192]{1,0:T(8,128)(2,1)} %q_ref, ...), custom_call_target="tpu_custom_call" | custom-call | tf_op jit(solution)/shard_map/pack_rows/pallas_call | solution.py:242
  17.5 1.8 %join.1.refs_7_ = bf16[2,768,128]{2,1,0:T(8,128)(2,1)} custom-call(bf16[2,96,128]{2,1,0:T(8,128)(2,1)} %get-tuple-element.77.refs_0_, bf16[2,96,128]{2,1,0:T(8,128)(2,1)} %copy-done.19, bf16[2,96,128]{2,1,0:T(8,128)(2,1)} %copy-done.20, bf16[2,96,128]{2,1,0:T(8,128)(2,1)} %copy-done.21, bf16[2,96,128]{2,1,0:T(8,128)(2,1)} %copy-done.22, ...), custom_call_target="tpu_custom_call" | custom-call | tf_op jit(solution)/shard_map/join/pallas_call | solution.py:213
  19.3 3.5 %collective-permute-start.12 = (bf16[2,768,128]{2,1,0:T(8,128)(2,1)}, bf16[2,768,128]{2,1,0:T(8,128)(2,1)S(1)}, u32[]{:S(2)}, u32[]{:S(2)}) collective-permute-start(bf16[2,768,128]{2,1,0:T(8,128)(2,1)} %join.1.refs_7_), channel_id=1, source_target_pairs={{0,8},{2,10},{4,12},{6,14},{8,16},{10,18},{12,20},{14,22},{16,24},... | collective-permute-start | bytes 1179656 | tf_op jit(solution)/shard_map/ppermute | solution.py:564
  24.6 4.0 %collective-permute-start.16 = (bf16[96,2048]{1,0:T(8,128)(2,1)}, bf16[96,2048]{1,0:T(8,128)(2,1)S(1)}, u32[]{:S(2)}, u32[]{:S(2)}) collective-permute-start(bf16[96,2048]{1,0:T(8,128)(2,1)} %get-tuple-element.97), channel_id=1, source_target_pairs={{0,6},{2,4},{4,2},{6,0},{8,14},{10,12},{12,10},{14,8},{16,22},{18,... | collective-permute-start | bytes 1179656 | tf_op jit(solution)/shard_map/ppermute | solution.py:592
  30.1 1.7 %collective-permute-done.12.refs_8_ = bf16[2,768,128]{2,1,0:T(8,128)(2,1)S(1)} collective-permute-done((bf16[2,768,128]{2,1,0:T(8,128)(2,1)}, bf16[2,768,128]{2,1,0:T(8,128)(2,1)S(1)}, u32[]{:S(2)}, u32[]{:S(2)}) %collective-permute-start.12) | collective-permute-done | bytes 393248 | tf_op jit(solution)/shard_map/ppermute | solution.py:564
  31.8 6.3 %collective-permute-start.13 = (bf16[2,192,128]{2,1,0:T(8,128)(2,1)S(1)}, bf16[2,192,128]{2,1,0:T(8,128)(2,1)S(1)}, u32[]{:S(2)}, u32[]{:S(2)}) collective-permute-start(bf16[2,192,128]{2,1,0:T(8,128)(2,1)S(1)} %slice.16), channel_id=1, source_target_pairs={{0,24},{2,26},{4,28},{6,30},{1,25},{3,27},{5,29},{7,31}} | collective-permute-start | bytes 294920 | tf_op jit(solution)/shard_map/ppermute | solution.py:633
  38.1 1.3 collective-permute-start.14
  39.5 1.4 copy-done.1
  40.9 1.4 copy-done.3
  43.2 7.8 %hyena.2 = (bf16[192,4096]{1,0:T(8,128)(2,1)}, bf16[192,4096]{1,0:T(8,128)(2,1)}, bf16[192,4096]{1,0:T(8,128)(2,1)}, bf16[192,4096]{1,0:T(8,128)(2,1)}) custom-call(bf16[192,4096]{1,0:T(8,128)(2,1)S(1)} %copy-done, bf16[192,4096]{1,0:T(8,128)(2,1)S(1)} %copy-done.1, bf16[192,4096]{1,0:T(8,128)(2,1)S(1)} %copy-done.3, bf16[192,4096]{1,0:T(8,128)(2,1)} %grad_ref.3, ...), custom_call_target="tpu_custom_call" | custom-call | flops 5505024000 | bytes 6291456 | tf_op jit(solution)/shard_map/hyena/pallas_call | solution.py:127
  51.0 1.6 %collective-permute-start = (bf16[96,2048]{1,0:T(8,128)(2,1)S(1)}, bf16[96,2048]{1,0:T(8,128)(2,1)S(1)}, u32[]{:S(2)}, u32[]{:S(2)}) collective-permute-start(bf16[96,2048]{1,0:T(8,128)(2,1)S(1)} %copy-done.28), channel_id=1, source_target_pairs={{0,4},{2,6},{4,0},{6,2},{8,12},{10,14},{12,8},{14,10},{16,20},{18,... | collective-permute-start | bytes 1179656 | tf_op jit(solution)/shard_map/ppermute | solution.py:592
  52.6 1.4 collective-permute-start.1
  54.8 11.3 %attention.2 = (bf16[192,2048]{1,0:T(8,128)(2,1)S(1)}, bf16[192,2048]{1,0:T(8,128)(2,1)S(1)}, bf16[2,192,128]{2,1,0:T(8,128)(2,1)S(1)}, bf16[2,768,128]{2,1,0:T(...) custom-call(s32[5]{0:T(128)S(1)} %stack.10.refs_0_, s32[16]{0:T(128)S(1)} %copy-done.17, ...), custom_call_target="tpu_custom_call" | custom-call | flops 48318382080 | bytes 12582912 | tf_op jit(solution)/shard_map/attention/pallas_call | solution.py:452
  66.0 1.3 collective-permute-start.19
  67.3 4.7 %collective-permute-done.1.refs_3_ = bf16[96,2048]{1,0:T(8,128)(2,1)S(1)} collective-permute-done((bf16[96,2048]{1,0:T(8,128)(2,1)S(1)}, bf16[96,2048]{1,0:T(8,128)(2,1)S(1)}, u32[]{:S(2)}, u32[]{:S(2)}) %collective-permute-start.1) | collective-permute-done | bytes 393248 | tf_op jit(solution)/shard_map/ppermute | solution.py:592
  72.0 1.4 %collective-permute-done.3.refs_5_ = bf16[96,2048]{1,0:T(8,128)(2,1)S(1)} collective-permute-done((bf16[96,2048]{1,0:T(8,128)(2,1)S(1)}, bf16[96,2048]{1,0:T(8,128)(2,1)S(1)}, u32[]{:S(2)}, u32[]{:S(2)}) %collective-permute-start.3) | collective-permute-done | bytes 393248 | tf_op jit(solution)/shard_map/ppermute | solution.py:592
  74.4 14.2 %attention.3 = (bf16[192,2048]{1,0:T(8,128)(2,1)}, bf16[192,2048]{1,0:T(8,128)(2,1)}, bf16[2,192,128]{2,1,0:T(8,128)(2,1)S(1)}, bf16[2,768,128]{2,1,0:T(8,128)(2...) custom-call(s32[5]{0:T(128)S(1)} %stack.10.refs_0_, s32[16]{0:T(128)S(1)} %copy-done.17, ...), custom_call_target="tpu_custom_call" | custom-call | flops 48318382080 | bytes 12582912 | tf_op jit(solution)/shard_map/attention/pallas_call | solution.py:452
  88.7 2.0 %collective-permute-start.23 = (bf16[192,2048]{1,0:T(8,128)(2,1)}, bf16[192,2048]{1,0:T(8,128)(2,1)}, u32[]{:S(2)}, u32[]{:S(2)}) collective-permute-start(bf16[192,2048]{1,0:T(8,128)(2,1)} %get-tuple-element.119), channel_id=1, source_target_pairs={{0,4},{2,6},{4,0},{6,2},{8,12},{10,14},{12,8},{14,10},{16,20},{18,... | collective-permute-start | bytes 2359304 | tf_op jit(solution)/shard_map/ppermute | solution.py:570
  90.7 1.5 %collective-permute-start.20 = (bf16[2,768,128]{2,1,0:T(8,128)(2,1)S(1)}, bf16[2,768,128]{2,1,0:T(8,128)(2,1)S(1)}, u32[]{:S(2)}, u32[]{:S(2)}) collective-permute-start(bf16[2,768,128]{2,1,0:T(8,128)(2,1)S(1)} %get-tuple-element.109), channel_id=1, source_target_pairs={{8,0},{10,2},{12,4},{14,6},{16,8},{18,10},{20,12},{22,14},{24,16},... | collective-permute-start | bytes 1179656 | tf_op jit(solution)/shard_map/ppermute | solution.py:567
  92.2 7.9 %hyena.3 = (bf16[192,4096]{1,0:T(8,128)(2,1)}, bf16[192,4096]{1,0:T(8,128)(2,1)}, bf16[192,4096]{1,0:T(8,128)(2,1)}, bf16[192,4096]{1,0:T(8,128)(2,1)}) custom-call(bf16[192,4096]{1,0:T(8,128)(2,1)S(1)} %copy-done, bf16[192,4096]{1,0:T(8,128)(2,1)S(1)} %copy-done.2, ...), custom_call_target="tpu_custom_call", output_to_operand_aliasing={{0}: (8, {}), {1}: (9, {}), {2}: (10, {}), {3}: (11, {})} | custom-call | flops 5505024000 | bytes 6291456 | tf_op jit(solution)/shard_map/hyena/pallas_call | solution.py:127
  100.1 4.8 %collective-permute-done.20 = bf16[2,768,128]{2,1,0:T(8,128)(2,1)S(1)} collective-permute-done((bf16[2,768,128]{2,1,0:T(8,128)(2,1)S(1)}, bf16[2,768,128]{2,1,0:T(8,128)(2,1)S(1)}, u32[]{:S(2)}, u32[]{:S(2)}) %collective-permute-start.20) | collective-permute-done | bytes 393248 | tf_op jit(solution)/shard_map/ppermute | solution.py:567
  105.0 1.4 collective-permute-start.21
  106.5 1.3 collective-permute-start.24
  109.0 3.2 %settle.1 = (bf16[192,4096]{1,0:T(8,128)(2,1)}, bf16[192,4096]{1,0:T(8,128)(2,1)}) custom-call(bf16[192,2048]{1,0:T(8,128)(2,1)S(1)} %get-tuple-element.117.refs_0_, bf16[192,2048]{1,0:T(8,128)(2,1)} %collective-permute-done.22.refs_1_, bf16[192,2048]{1,0:T(8,128)(2,1)} %collective-permute-done.23.refs_2_, bf16[192,2048]{1,0:T(8,128)(2,1)S(1)} %copy-done.6), custom_call_target="tpu_custom_call" | custom-call | tf_op jit(solution)/shard_map/settle/pallas_call | solution.py:505
  112.2 20.8 %collective-permute-done.21 = bf16[2,768,128]{2,1,0:T(8,128)(2,1)S(1)} collective-permute-done((bf16[2,768,128]{2,1,0:T(8,128)(2,1)S(1)}, bf16[2,768,128]{2,1,0:T(8,128)(2,1)S(1)}, u32[]{:S(2)}, u32[]{:S(2)}) %collective-permute-start.21) | collective-permute-done | bytes 393248 | tf_op jit(solution)/shard_map/ppermute | solution.py:567
  133.2 4.1 %collective-permute-done.24 = bf16[2,192,128]{2,1,0:T(8,128)(2,1)S(1)} collective-permute-done((bf16[2,192,128]{2,1,0:T(8,128)(2,1)}, bf16[2,192,128]{2,1,0:T(8,128)(2,1)S(1)}, u32[]{:S(2)}, u32[]{:S(2)}) %collective-permute-start.24) | collective-permute-done | bytes 98336 | tf_op jit(solution)/shard_map/ppermute | solution.py:670
  138.5 1.3 collective-permute-start.27
  139.8 2.9 %collective-permute-done.25 = bf16[2,192,128]{2,1,0:T(8,128)(2,1)S(1)} collective-permute-done((bf16[2,192,128]{2,1,0:T(8,128)(2,1)S(1)}, bf16[2,192,128]{2,1,0:T(8,128)(2,1)S(1)}, u32[]{:S(2)}, u32[]{:S(2)}) %collective-permute-start.25) | collective-permute-done | bytes 98336 | tf_op jit(solution)/shard_map/ppermute | solution.py:570
  (101 shorter events, 14.3 us)
Async XLA Ops:
  3.1 5.9 %collective-permute-start.10 = (bf16[2,96,128]{2,1,0:T(8,128)(2,1)}, bf16[2,96,128]{2,1,0:T(8,128)(2,1)S(1)}, u32[]{:S(2)}, u32[]{:S(2)}) collective-permute-start(bf16[2,96,128]{2,1,0:T(8,128)(2,1)} %get-tuple-element.84), channel_id=1, source_target_pairs={{0,7},{2,5},{4,3},{6,1},{8,15},{10,13},{12,11},{14,9},{16,23},{18,... | collective-permute-start | bytes 147464 | tf_op jit(solution)/shard_map/ppermute | solution.py:592
  6.4 4.5 %collective-permute-start.4 = (bf16[2,96,128]{2,1,0:T(8,128)(2,1)}, bf16[2,96,128]{2,1,0:T(8,128)(2,1)S(1)}, u32[]{:S(2)}, u32[]{:S(2)}) collective-permute-start(bf16[2,96,128]{2,1,0:T(8,128)(2,1)} %get-tuple-element.78), channel_id=1, source_target_pairs={{0,2},{2,0},{4,6},{6,4},{8,10},{10,8},{12,14},{14,12},{16,18},{18,... | collective-permute-start | bytes 147464 | tf_op jit(solution)/shard_map/ppermute | solution.py:592
  7.1 9.1 %collective-permute-start.5 = (bf16[2,96,128]{2,1,0:T(8,128)(2,1)}, bf16[2,96,128]{2,1,0:T(8,128)(2,1)S(1)}, u32[]{:S(2)}, u32[]{:S(2)}) collective-permute-start(bf16[2,96,128]{2,1,0:T(8,128)(2,1)} %get-tuple-element.79), channel_id=1, source_target_pairs={{0,4},{2,6},{4,0},{6,2},{8,12},{10,14},{12,8},{14,10},{16,20},{18,... | collective-permute-start | bytes 147464 | tf_op jit(solution)/shard_map/ppermute | solution.py:592
  7.6 8.6 %collective-permute-start.6 = (bf16[2,96,128]{2,1,0:T(8,128)(2,1)}, bf16[2,96,128]{2,1,0:T(8,128)(2,1)S(1)}, u32[]{:S(2)}, u32[]{:S(2)}) collective-permute-start(bf16[2,96,128]{2,1,0:T(8,128)(2,1)} %get-tuple-element.80), channel_id=1, source_target_pairs={{0,6},{2,4},{4,2},{6,0},{8,14},{10,12},{12,10},{14,8},{16,22},{18,... | collective-permute-start | bytes 147464 | tf_op jit(solution)/shard_map/ppermute | solution.py:592
  8.4 7.8 %collective-permute-start.7 = (bf16[2,96,128]{2,1,0:T(8,128)(2,1)}, bf16[2,96,128]{2,1,0:T(8,128)(2,1)S(1)}, u32[]{:S(2)}, u32[]{:S(2)}) collective-permute-start(bf16[2,96,128]{2,1,0:T(8,128)(2,1)} %get-tuple-element.81), channel_id=1, source_target_pairs={{0,1},{2,3},{4,5},{6,7},{8,9},{10,11},{12,13},{14,15},{16,17},{18,... | collective-permute-start | bytes 147464 | tf_op jit(solution)/shard_map/ppermute | solution.py:592
  9.0 7.3 %collective-permute-start.8 = (bf16[2,96,128]{2,1,0:T(8,128)(2,1)}, bf16[2,96,128]{2,1,0:T(8,128)(2,1)S(1)}, u32[]{:S(2)}, u32[]{:S(2)}) collective-permute-start(bf16[2,96,128]{2,1,0:T(8,128)(2,1)} %get-tuple-element.82), channel_id=1, source_target_pairs={{0,3},{2,1},{4,7},{6,5},{8,11},{10,9},{12,15},{14,13},{16,19},{18,... | collective-permute-start | bytes 147464 | tf_op jit(solution)/shard_map/ppermute | solution.py:592
  10.9 5.4 %collective-permute-start.9 = (bf16[2,96,128]{2,1,0:T(8,128)(2,1)}, bf16[2,96,128]{2,1,0:T(8,128)(2,1)S(1)}, u32[]{:S(2)}, u32[]{:S(2)}) collective-permute-start(bf16[2,96,128]{2,1,0:T(8,128)(2,1)} %get-tuple-element.83), channel_id=1, source_target_pairs={{0,5},{2,7},{4,1},{6,3},{8,13},{10,15},{12,9},{14,11},{16,21},{18,... | collective-permute-start | bytes 147464 | tf_op jit(solution)/shard_map/ppermute | solution.py:592
  12.3 27.1 %copy-start = (bf16[192,4096]{1,0:T(8,128)(2,1)S(1)}, bf16[192,4096]{1,0:T(8,128)(2,1)}, u32[]{:S(2)}) copy-start(bf16[192,4096]{1,0:T(8,128)(2,1)} %gate_ref.3) | copy-start | bytes 4718596
  12.3 27.1 %copy-start.16 = (f32[7,256]{1,0:T(8,128)S(1)}, f32[7,256]{1,0:T(8,128)}, u32[]{:S(2)}) copy-start(f32[7,256]{1,0:T(8,128)} %long_ref.3) | copy-start | bytes 21508
  19.3 12.5 %collective-permute-start.12 = (bf16[2,768,128]{2,1,0:T(8,128)(2,1)}, bf16[2,768,128]{2,1,0:T(8,128)(2,1)S(1)}, u32[]{:S(2)}, u32[]{:S(2)}) collective-permute-start(bf16[2,768,128]{2,1,0:T(8,128)(2,1)} %join.1.refs_7_), channel_id=1, source_target_pairs={{0,8},{2,10},{4,12},{6,14},{8,16},{10,18},{12,20},{14,22},{16,24},... | collective-permute-start | bytes 1179656 | tf_op jit(solution)/shard_map/ppermute | solution.py:564
  22.8 6.8 %collective-permute-start.11 = (bf16[32,4096]{1,0:T(8,128)(2,1)}, bf16[32,4096]{1,0:T(8,128)(2,1)S(1)}, u32[]{:S(2)}, u32[]{:S(2)}) collective-permute-start(bf16[32,4096]{1,0:T(8,128)(2,1)} %get-tuple-element.89), channel_id=1, source_target_pairs={{0,2},{2,0},{4,6},{6,4},{8,10},{10,8},{12,14},{14,12},{16,18},{18,... | collective-permute-start | bytes 786440 | tf_op jit(solution)/shard_map/ppermute | solution.py:579
  22.9 15.2 %collective-permute-start.15 = (bf16[32,4096]{1,0:T(8,128)(2,1)}, bf16[32,4096]{1,0:T(8,128)(2,1)S(1)}, u32[]{:S(2)}, u32[]{:S(2)}) collective-permute-start(bf16[32,4096]{1,0:T(8,128)(2,1)} %get-tuple-element.94), channel_id=1, source_target_pairs={{2,4},{4,2},{6,8},{8,6},{10,12},{12,10},{14,16},{16,14},{18,20},{2... | collective-permute-start | bytes 786440 | tf_op jit(solution)/shard_map/ppermute | solution.py:580
  23.7 31.0 %copy-start.17 = (s32[16]{0:T(128)S(1)}, s32[16]{0:T(128)}, u32[]{:S(2)}) copy-start(s32[16]{0:T(128)} %refs_1_.5) | copy-start | bytes 196
  24.6 28.0 %collective-permute-start.16 = (bf16[96,2048]{1,0:T(8,128)(2,1)}, bf16[96,2048]{1,0:T(8,128)(2,1)S(1)}, u32[]{:S(2)}, u32[]{:S(2)}) collective-permute-start(bf16[96,2048]{1,0:T(8,128)(2,1)} %get-tuple-element.97), channel_id=1, source_target_pairs={{0,6},{2,4},{4,2},{6,0},{8,14},{10,12},{12,10},{14,8},{16,22},{18,... | collective-permute-start | bytes 1179656 | tf_op jit(solution)/shard_map/ppermute | solution.py:592
  28.6 25.5 %collective-permute-start.17 = (bf16[96,2048]{1,0:T(8,128)(2,1)}, bf16[96,2048]{1,0:T(8,128)(2,1)S(1)}, u32[]{:S(2)}, u32[]{:S(2)}) collective-permute-start(bf16[96,2048]{1,0:T(8,128)(2,1)} %get-tuple-element.98), channel_id=1, source_target_pairs={{0,7},{2,5},{4,3},{6,1},{8,15},{10,13},{12,11},{14,9},{16,23},{18,... | collective-permute-start | bytes 1179656 | tf_op jit(solution)/shard_map/ppermute | solution.py:592
  29.6 24.5 %collective-permute-start.18 = (bf16[96,2048]{1,0:T(8,128)(2,1)}, bf16[96,2048]{1,0:T(8,128)(2,1)S(1)}, u32[]{:S(2)}, u32[]{:S(2)}) collective-permute-start(bf16[96,2048]{1,0:T(8,128)(2,1)} %get-tuple-element.100), channel_id=1, source_target_pairs={{0,1},{2,3},{4,5},{6,7},{8,9},{10,11},{12,13},{14,15},{16,17},{18,... | collective-permute-start | bytes 1179656 | tf_op jit(solution)/shard_map/ppermute | solution.py:592
  31.8 22.9 %copy-start.9 = (bf16[2,768,128]{2,1,0:T(8,128)(2,1)}, bf16[2,768,128]{2,1,0:T(8,128)(2,1)S(1)}, u32[]{:S(2)}) copy-start(bf16[2,768,128]{2,1,0:T(8,128)(2,1)S(1)} %collective-permute-done.12.refs_8_) | copy-start | bytes 1179652
  31.8 22.9 %collective-permute-start.13 = (bf16[2,192,128]{2,1,0:T(8,128)(2,1)S(1)}, bf16[2,192,128]{2,1,0:T(8,128)(2,1)S(1)}, u32[]{:S(2)}, u32[]{:S(2)}) collective-permute-start(bf16[2,192,128]{2,1,0:T(8,128)(2,1)S(1)} %slice.16), channel_id=1, source_target_pairs={{0,24},{2,26},{4,28},{6,30},{1,25},{3,27},{5,29},{7,31}} | collective-permute-start | bytes 294920 | tf_op jit(solution)/shard_map/ppermute | solution.py:633
  38.1 12.9 %collective-permute-start.14 = (bf16[2,768,128]{2,1,0:T(8,128)(2,1)S(1)}, bf16[2,768,128]{2,1,0:T(8,128)(2,1)S(1)}, u32[]{:S(2)}, u32[]{:S(2)}) collective-permute-start(bf16[2,768,128]{2,1,0:T(8,128)(2,1)S(1)} %collective-permute-done.12.refs_8_), channel_id=1, source_target_pairs={{0,8},{2,10},{4,12},{6,14},{8,16},{10,18},{12,20},{14,22},{16,24},... | collective-permute-start | bytes 1179656 | tf_op jit(solution)/shard_map/ppermute | solution.py:564
  51.0 16.3 %collective-permute-start = (bf16[96,2048]{1,0:T(8,128)(2,1)S(1)}, bf16[96,2048]{1,0:T(8,128)(2,1)S(1)}, u32[]{:S(2)}, u32[]{:S(2)}) collective-permute-start(bf16[96,2048]{1,0:T(8,128)(2,1)S(1)} %copy-done.28), channel_id=1, source_target_pairs={{0,4},{2,6},{4,0},{6,2},{8,12},{10,14},{12,8},{14,10},{16,20},{18,... | collective-permute-start | bytes 1179656 | tf_op jit(solution)/shard_map/ppermute | solution.py:592
  52.6 19.3 %collective-permute-start.1 = (bf16[96,2048]{1,0:T(8,128)(2,1)S(1)}, bf16[96,2048]{1,0:T(8,128)(2,1)S(1)}, u32[]{:S(2)}, u32[]{:S(2)}) collective-permute-start(bf16[96,2048]{1,0:T(8,128)(2,1)S(1)} %copy-done.27), channel_id=1, source_target_pairs={{0,5},{2,7},{4,1},{6,3},{8,13},{10,15},{12,9},{14,11},{16,21},{18,... | collective-permute-start | bytes 1179656 | tf_op jit(solution)/shard_map/ppermute | solution.py:592
  54.1 17.9 %collective-permute-start.2 = (bf16[96,2048]{1,0:T(8,128)(2,1)S(1)}, bf16[96,2048]{1,0:T(8,128)(2,1)S(1)}, u32[]{:S(2)}, u32[]{:S(2)}) collective-permute-start(bf16[96,2048]{1,0:T(8,128)(2,1)S(1)} %copy-done.26), channel_id=1, source_target_pairs={{0,2},{2,0},{4,6},{6,4},{8,10},{10,8},{12,14},{14,12},{16,18},{18,... | collective-permute-start | bytes 1179656 | tf_op jit(solution)/shard_map/ppermute | solution.py:592
  54.1 19.3 %collective-permute-start.3 = (bf16[96,2048]{1,0:T(8,128)(2,1)S(1)}, bf16[96,2048]{1,0:T(8,128)(2,1)S(1)}, u32[]{:S(2)}, u32[]{:S(2)}) collective-permute-start(bf16[96,2048]{1,0:T(8,128)(2,1)S(1)} %copy-done.25), channel_id=1, source_target_pairs={{0,3},{2,1},{4,7},{6,5},{8,11},{10,9},{12,15},{14,13},{16,19},{18,... | collective-permute-start | bytes 1179656 | tf_op jit(solution)/shard_map/ppermute | solution.py:592
  66.0 24.7 %collective-permute-start.19 = (bf16[192,2048]{1,0:T(8,128)(2,1)S(1)}, bf16[192,2048]{1,0:T(8,128)(2,1)S(1)}, u32[]{:S(2)}, u32[]{:S(2)}) collective-permute-start(bf16[192,2048]{1,0:T(8,128)(2,1)S(1)} %get-tuple-element.107), channel_id=1, source_target_pairs={{0,6},{2,4},{4,2},{6,0},{8,14},{10,12},{12,10},{14,8},{16,22},{18,... | collective-permute-start | bytes 2359304 | tf_op jit(solution)/shard_map/ppermute | solution.py:570
  88.7 19.1 %collective-permute-start.22 = (bf16[192,2048]{1,0:T(8,128)(2,1)}, bf16[192,2048]{1,0:T(8,128)(2,1)}, u32[]{:S(2)}, u32[]{:S(2)}) collective-permute-start(bf16[192,2048]{1,0:T(8,128)(2,1)} %get-tuple-element.118), channel_id=1, source_target_pairs={{0,2},{2,0},{4,6},{6,4},{8,10},{10,8},{12,14},{14,12},{16,18},{18,... | collective-permute-start | bytes 2359304 | tf_op jit(solution)/shard_map/ppermute | solution.py:570
  88.7 20.3 %collective-permute-start.23 = (bf16[192,2048]{1,0:T(8,128)(2,1)}, bf16[192,2048]{1,0:T(8,128)(2,1)}, u32[]{:S(2)}, u32[]{:S(2)}) collective-permute-start(bf16[192,2048]{1,0:T(8,128)(2,1)} %get-tuple-element.119), channel_id=1, source_target_pairs={{0,4},{2,6},{4,0},{6,2},{8,12},{10,14},{12,8},{14,10},{16,20},{18,... | collective-permute-start | bytes 2359304 | tf_op jit(solution)/shard_map/ppermute | solution.py:570
  90.7 14.2 %collective-permute-start.20 = (bf16[2,768,128]{2,1,0:T(8,128)(2,1)S(1)}, bf16[2,768,128]{2,1,0:T(8,128)(2,1)S(1)}, u32[]{:S(2)}, u32[]{:S(2)}) collective-permute-start(bf16[2,768,128]{2,1,0:T(8,128)(2,1)S(1)} %get-tuple-element.109), channel_id=1, source_target_pairs={{8,0},{10,2},{12,4},{14,6},{16,8},{18,10},{20,12},{22,14},{24,16},... | collective-permute-start | bytes 1179656 | tf_op jit(solution)/shard_map/ppermute | solution.py:567
  105.0 28.0 %collective-permute-start.21 = (bf16[2,768,128]{2,1,0:T(8,128)(2,1)S(1)}, bf16[2,768,128]{2,1,0:T(8,128)(2,1)S(1)}, u32[]{:S(2)}, u32[]{:S(2)}) collective-permute-start(bf16[2,768,128]{2,1,0:T(8,128)(2,1)S(1)} %add_convert_fusion), channel_id=1, source_target_pairs={{8,0},{10,2},{12,4},{14,6},{16,8},{18,10},{20,12},{22,14},{24,16},... | collective-permute-start | bytes 1179656 | tf_op jit(solution)/shard_map/ppermute | solution.py:567
  106.5 30.8 %collective-permute-start.24 = (bf16[2,192,128]{2,1,0:T(8,128)(2,1)}, bf16[2,192,128]{2,1,0:T(8,128)(2,1)S(1)}, u32[]{:S(2)}, u32[]{:S(2)}) collective-permute-start(bf16[2,192,128]{2,1,0:T(8,128)(2,1)} %copy-done.15), channel_id=1, source_target_pairs={{24,0},{26,2},{28,4},{30,6},{25,1},{27,3},{29,5},{31,7}} | collective-permute-start | bytes 294920 | tf_op jit(solution)/shard_map/ppermute | solution.py:670
  137.8 4.8 %collective-permute-start.25 = (bf16[2,192,128]{2,1,0:T(8,128)(2,1)S(1)}, bf16[2,192,128]{2,1,0:T(8,128)(2,1)S(1)}, u32[]{:S(2)}, u32[]{:S(2)}) collective-permute-start(bf16[2,192,128]{2,1,0:T(8,128)(2,1)S(1)} %get-tuple-element.138), channel_id=1, source_target_pairs={{0,6},{2,4},{4,2},{6,0},{8,14},{10,12},{12,10},{14,8},{16,22},{18,... | collective-permute-start | bytes 294920 | tf_op jit(solution)/shard_map/ppermute | solution.py:570
  137.9 5.7 %collective-permute-start.26 = (bf16[2,192,128]{2,1,0:T(8,128)(2,1)S(1)}, bf16[2,192,128]{2,1,0:T(8,128)(2,1)S(1)}, u32[]{:S(2)}, u32[]{:S(2)}) collective-permute-start(bf16[2,192,128]{2,1,0:T(8,128)(2,1)S(1)} %get-tuple-element.139), channel_id=1, source_target_pairs={{0,4},{2,6},{4,0},{6,2},{8,12},{10,14},{12,8},{14,10},{16,20},{18,... | collective-permute-start | bytes 294920 | tf_op jit(solution)/shard_map/ppermute | solution.py:570
  138.5 5.1 %collective-permute-start.27 = (bf16[2,192,128]{2,1,0:T(8,128)(2,1)S(1)}, bf16[2,192,128]{2,1,0:T(8,128)(2,1)S(1)}, u32[]{:S(2)}, u32[]{:S(2)}) collective-permute-start(bf16[2,192,128]{2,1,0:T(8,128)(2,1)S(1)} %get-tuple-element.137), channel_id=1, source_target_pairs={{0,2},{2,0},{4,6},{6,4},{8,10},{10,8},{12,14},{14,12},{16,18},{18,... | collective-permute-start | bytes 294920 | tf_op jit(solution)/shard_map/ppermute | solution.py:570
  (25 other events, 191.1 us)
